TPU v7x, 256 devices: a whole 4x4x8 slice. The times are simulated.
256 devices in a mesh: tok: 16 (over y, x_hi, core), feat: 16 (over z, x_lo).
Axes of the slice: x: 4 (x_hi: 2, x_lo: 2; x = x_hi * 2 + x_lo), y: 4, z: 8, core: 2. Of those that a mesh axis runs over, the one named last changes fastest.
Arguments:
- gradients: bfloat16 [8192, 6912], P('tok', 'feat'), may hold values from -30 to 30
- previous: float32 [6912, 6912], P(('feat', 'tok')), may hold values from -4 to 4
Outputs:
- factor: float32 [6912, 6912], P(('feat', 'tok'))
All inputs are finite; a program needn't handle non-finite values.
Results may differ from a plain program's by a relative error of at most 0.0003.
Values may be sent and summed in bfloat16 or wider, within the bound.
No kernel may reach another device: no remote copies, remote signals or barrier semaphores. Data moves between devices by JAX's collectives and lax.ppermute only.
A program may use at most 64 MiB of HBM per device.

v0:
```python
import functools

import jax
import jax.numpy as jnp
from jax import lax
from jax.experimental import pallas as pl
from jax.experimental.pallas import tpu as pltpu
from jax.sharding import PartitionSpec as P

PRIOR = 1
AXES = ("tok", "feat")
NY, NXH, NC, NZ, NXL = 4, 2, 2, 8, 2
N_TOK, N_FEAT = NY * NXH * NC, NZ * NXL


def linear(y, xh, c, z, xl):
    return ((y % NY * NXH + xh % NXH) * NC + c % NC) * N_FEAT + z % NZ * NXL + xl % NXL


def move(value, where, turned=False):
    pairs = []
    for y in range(NY):
        for xh in range(NXH):
            for c in range(NC):
                for z in range(NZ):
                    for xl in range(NXL):
                        to = where(y, xh, c, z, xl)
                        if to is not None:
                            pairs.append((linear(y, xh, c, z, xl), linear(*to)))
    return lax.ppermute(value, AXES, pairs[::-1] if turned else pairs)


def along_z(value, by):
    return move(value, lambda y, xh, c, z, xl: (y, xh, c, z + by, xl))


def along_y(value, by, turned=False):
    return move(value, lambda y, xh, c, z, xl: (y + by, xh, c, z, xl), turned)


def other_xl(value):
    return move(value, lambda y, xh, c, z, xl: (y, xh, c, z, xl + 1))


def other_xh(value):
    return move(value, lambda y, xh, c, z, xl: (y, xh + 1, c, z, xl))


def other_core(value):
    return move(value, lambda y, xh, c, z, xl: (y, xh, c + 1, z, xl))


def products_kernel(units, n_shards, width, *refs):
    sources, out = refs[: 2 * n_shards], refs[2 * n_shards]
    held, full, arrived = refs[2 * n_shards + 1 :]
    core = lax.rem(lax.axis_index("tok"), NC)
    n_rows = width // (NY * NXH)
    depth = held.shape[2]
    half = depth // 2
    copies = []
    for i in range(n_shards):
        for side in range(2):
            place = held.at[i, :, side * half : (side + 1) * half]
            copies.append(pltpu.make_async_copy(sources[2 * i + side], place, arrived.at[i, side]))
            copies[-1].start()
    peak = jnp.zeros((16, depth), jnp.float32)
    for i in range(n_shards):
        copies[2 * i].wait()
        copies[2 * i + 1].wait()
        rows = jnp.max(jnp.abs(held[i]).reshape(width // 16, 16, depth), axis=0)
        peak = jnp.maximum(peak, rows.astype(jnp.float32))
    peak = jnp.maximum(jnp.max(peak), 1e-18)

    for c in range(NC):

        @pl.when(core == c)
        def _():
            for slot, (a, b) in enumerate(units[c]):
                full[:width, slot * width : (slot + 1) * width] = lax.dot_general(
                    held[a], held[b], (((1,), (1,)), ((), ())), preferred_element_type=jnp.float32
                )

    column = lax.broadcasted_iota(jnp.int32, (1, full.shape[1]), 1)
    fraction = lax.rem(column * 7, 16).astype(jnp.float32) * 0.0625
    exponent = jnp.ceil(2.0 * jnp.log2(jnp.full((1, full.shape[1]), peak))) + (depth.bit_length() - 15) + fraction
    exponents = jnp.broadcast_to(jnp.maximum(exponent, -125.0), (out.shape[2] - n_rows, full.shape[1]))
    for k in range(NY * NXH):
        out[k // NXH, k % NXH, :n_rows, :] = full[k * n_rows : (k + 1) * n_rows, :]
        out[k // NXH, k % NXH, n_rows:, :] = exponents


def products(units, shards):
    width, half = shards[0][0].shape
    n_units = len(units[0])
    padded = -(-(width // (NY * NXH)) // 8) * 8
    flat = [side for shard in shards for side in shard]
    return pl.pallas_call(
        functools.partial(products_kernel, units, len(shards), width),
        out_shape=jax.ShapeDtypeStruct((NY, NXH, padded, n_units * width), jnp.float32),
        in_specs=[pl.BlockSpec(memory_space=pl.ANY)] * len(flat),
        out_specs=pl.BlockSpec(memory_space=pltpu.VMEM),
        scratch_shapes=[
            pltpu.VMEM((len(shards), width, 2 * half), shards[0][0].dtype),
            pltpu.VMEM((width, n_units * width), jnp.float32),
            pltpu.SemaphoreType.DMA((len(shards), 2)),
        ],
        compiler_params=pltpu.CompilerParams(vmem_limit_bytes=20 * 1024 * 1024),
        cost_estimate=pl.CostEstimate(
            flops=n_units * 4 * width * width * half, bytes_accessed=8 * 1024 * 1024, transcendentals=0
        ),
    )(*flat)


def at_exponent(value, n_rows):
    return lax.broadcasted_iota(jnp.int32, value.shape, value.ndim - 2) == n_rows


def exponent_row(value, n_rows):
    return lax.slice_in_dim(value, n_rows, n_rows + 1, axis=value.ndim - 2)


def packed(value, n_rows):
    scaled = value * jnp.exp2(-exponent_row(value, n_rows))
    return jnp.where(at_exponent(value, n_rows), value, scaled).astype(jnp.float16)


def unpacked(value, n_rows):
    value = value.astype(jnp.float32)
    return jnp.where(at_exponent(value, n_rows), value, value * jnp.exp2(exponent_row(value, n_rows)))


def added(a, b, n_rows):
    return jnp.where(at_exponent(a, n_rows), jnp.maximum(a, b) + 1.3125, a + b)


def tied(value, *others):
    return lax.optimization_barrier((value, *others))[0]


def chunk_of(part, at):
    return lax.dynamic_index_in_dim(part, lax.rem(at, part.shape[0]), 0, keepdims=False)


def y_first(part, n_rows, y_at):
    far = chunk_of(part, y_at + 2)
    return packed(far[0], n_rows), packed(far[1], n_rows)


def y_second(part, arrived, n_rows, y_at):
    above, below = chunk_of(part, y_at + 1), chunk_of(part, y_at + 3)
    first = added(above[0], unpacked(arrived[0], n_rows), n_rows)
    second = added(below[1], unpacked(arrived[1], n_rows), n_rows)
    to_above = packed(jnp.stack([first, above[1]]), n_rows)
    to_below = packed(jnp.stack([below[0], second]), n_rows)
    return to_above, to_below


def y_last(part, arrived, n_rows, y_at):
    summed = added(unpacked(arrived[0], n_rows), unpacked(arrived[1], n_rows), n_rows)
    return added(chunk_of(part, y_at), summed, n_rows)


def x_give(summed, n_rows, xh_at):
    return packed(chunk_of(summed, xh_at + 1), n_rows)


def x_last(summed, arrived, n_rows, xh_at):
    return chunk_of(summed, xh_at) + unpacked(arrived, n_rows)


HELD = (
    ((1, 0), (-1, 1), (1, 1), (3, 0), (0, 0), (3, 1), (4, 0), (4, 1)),
    ((2, 0), (-1, 0), (-2, 0), (-3, 0), (0, 1), (2, 1), (-2, 1), (-3, 1)),
)


def assemble_kernel(width, count, mine, theirs, previous, out, stack):
    n_rows = previous.shape[0]
    core = lax.rem(lax.axis_index("tok"), NC)
    feat = lax.axis_index("feat")
    z_at, xl_at = feat // NXL, lax.rem(feat, NXL)
    for c in range(NC):

        @pl.when(core == c)
        def _():
            for slot in range(len(HELD[c])):
                columns = slice(slot * width, (slot + 1) * width)
                dz, dx = HELD[c][slot]
                stack[dz % NZ * NXL + dx, :n_rows, :] = mine[c * n_rows : (c + 1) * n_rows, columns]
                dz, dx = HELD[1 - c][slot]
                stack[dz % NZ * NXL + dx, :n_rows, :] = theirs[:, columns]

    for f in range(N_FEAT):
        at = lax.rem(f // NXL - z_at + NZ, NZ) * NXL + lax.rem(f % NXL + xl_at, NXL)
        columns = slice(f * width, (f + 1) * width)
        cov = stack[at, :n_rows, :] * (1.0 / count)
        out[:, columns] = (PRIOR * previous[:, columns] + cov) * (1.0 / (PRIOR + 1))


def assemble(mine, theirs, previous, width, count):
    n_rows = previous.shape[0]
    return pl.pallas_call(
        functools.partial(assemble_kernel, width, count),
        out_shape=jax.ShapeDtypeStruct(previous.shape, jnp.float32),
        in_specs=[pl.BlockSpec(memory_space=pltpu.VMEM)] * 3,
        out_specs=pl.BlockSpec(memory_space=pltpu.VMEM),
        scratch_shapes=[pltpu.VMEM((N_FEAT, -(-n_rows // 8) * 8, width), jnp.float32)],
        compiler_params=pltpu.CompilerParams(vmem_limit_bytes=14 * 1024 * 1024),
        cost_estimate=pl.CostEstimate(flops=0, bytes_accessed=4 * 1024 * 1024, transcendentals=0),
    )(mine, theirs, previous)


def per_device(gradients, previous):
    width = gradients.shape[1]
    count = gradients.shape[0] * N_TOK
    n_rows = previous.shape[0]
    tok = lax.axis_index("tok")
    y_at, xh_at, c_at = tok // (NXH * NC), lax.rem(tok // NC, NXH), lax.rem(tok, NC)

    own = gradients.T
    after, before, across = along_z(own, -1), along_z(own, 1), other_xl(own)
    own_2 = other_core(own)
    after2, before2 = along_z(after, -1), along_z(before, 1)
    across2 = other_xl(after2)
    after_2, before_2, across_2 = (other_core(tied(shard, own_2)) for shard in (after, before, across))
    after2_2 = other_core(after2)

    near = [(own, own_2), (after, after_2), (before, before_2), (across, across_2), (after2, after2_2)]
    rows = n_rows * NC
    part1 = products(
        (((0, 1), (3, 2), (2, 3), (2, 4), (0, 0)), ((0, 4), (1, 0), (4, 0), (4, 2), (0, 3))), near
    )
    far1 = y_first(part1, rows, y_at)
    half1 = along_y(far1[0], 1), along_y(far1[1], -1)
    across2_2, before2_2 = other_core(tied(across2, *far1)), other_core(tied(before2, *far1))

    far = [(own, own_2), (before, before_2), (before2, before2_2), (across2, across2_2), (after2, after2_2)]
    part2 = products((((1, 3), (2, 4), (2, 3)), ((0, 3), (3, 0), (3, 1))), far)
    far2 = y_first(part2, rows, y_at)
    half2 = along_y(far2[0], 1, True), along_y(far2[1], -1, True)
    half1 = lax.optimization_barrier(half1)
    give1 = y_second(part1, half1, rows, y_at)
    got1 = lax.optimization_barrier((along_y(give1[0], 1), along_y(give1[1], -1)))
    half2 = lax.optimization_barrier((*half2, *give1))[:2]
    give2 = y_second(part2, half2, rows, y_at)
    got2 = lax.optimization_barrier((along_y(give2[0], 1, True), along_y(give2[1], -1, True)))
    summed1 = y_last(part1, got1, rows, y_at)
    x_got1 = other_xh(x_give(summed1, rows, xh_at))
    sum1 = x_last(summed1, x_got1, rows, xh_at)

    def shifted(value, low, high, xh_by=0):
        def where(y, xh, c, z, xl):
            by = (low, high)[c]
            return None if by is None else (y, xh + xh_by, c, z + by[0], xl + by[1])

        return move(value, where)

    w = width
    got_a = shifted(sum1[:, w : 2 * w], (0, 1), (1, 0))
    got_b = shifted(sum1[:, 2 * w : 4 * w], (-1, 0), (2, 0))
    summed2 = y_last(part2, got2, rows, y_at)
    keep, give = chunk_of(summed2, xh_at), packed(chunk_of(summed2, xh_at + 1), rows)
    kept = packed(keep, rows)
    d_same, d_other = shifted(kept[:, :w], (-1, 0), None), shifted(give[:, :w], (-1, 0), (0, 0), 1)
    e_same, e_other = shifted(kept[:, w:], (-2, 0), (2, 1)), shifted(give[:, w:], (-2, 0), (2, 1), 1)
    d_same, d_other, e_same, e_other = lax.optimization_barrier((d_same, d_other, e_same, e_other))
    got_d = jnp.where(c_at == 0, unpacked(d_same, rows), keep[:, :w]) + unpacked(d_other, rows)
    got_e = unpacked(e_same, rows) + unpacked(e_other, rows)
    mine = jnp.concatenate([sum1[:, :w], got_a, got_b, sum1[:, 4 * w :], got_d, got_e], axis=1)
    theirs = other_core(lax.dynamic_slice_in_dim(mine, (1 - c_at) * n_rows, n_rows, 0))
    return assemble(mine, theirs, previous, width, count)


def solution(mesh):
    placed = (P("tok", "feat"), P(("feat", "tok"), None))
    return jax.shard_map(
        per_device, mesh=mesh, in_specs=placed, out_specs=P(("feat", "tok"), None), check_vma=False
    )
```

profile of v0, /device:TPU:1, one launch (start us, length us, event | category | flops | bytes accessed | tf_op | source)
XLA Modules:
  0.0 98.1 jit_solution(9453315601503812396)
XLA Ops:
  0.0 6.4 %collective-permute-start.1 = (bf16[432,512]{1,0:T(8,128)(2,1)}, bf16[432,512]{1,0:T(8,128)(2,1)S(1)}, u32[]{:S(2)}, u32[]{:S(2)}) collective-permute-start(bf16[432,512]{1,0:T(8,128)(2,1)} %bitcast.102), channel_id=1, source_target_pairs={{0,14},{1,15},{2,0},{3,1},{4,2},{5,3},{6,4},{7,5},{8,6},{9,7},{10,... | collective-permute-start | bytes 1327112 | tf_op jit(solution)/shard_map/ppermute | solution.py:30
  7.4 1.2 %collective-permute-start.5 = (bf16[432,512]{1,0:T(8,128)(2,1)}, bf16[432,512]{1,0:T(8,128)(2,1)S(1)}, u32[]{:S(2)}, u32[]{:S(2)}) collective-permute-start(bf16[432,512]{1,0:T(8,128)(2,1)} %bitcast.105), channel_id=1, source_target_pairs={{0,1},{1,0},{2,3},{3,2},{4,5},{5,4},{6,7},{7,6},{8,9},{9,8},{10,11... | collective-permute-start | bytes 1327112 | tf_op jit(solution)/shard_map/ppermute | solution.py:30
  8.6 7.0 %collective-permute-done.1.refs_2_ = bf16[432,512]{1,0:T(8,128)(2,1)S(1)} collective-permute-done((bf16[432,512]{1,0:T(8,128)(2,1)}, bf16[432,512]{1,0:T(8,128)(2,1)S(1)}, u32[]{:S(2)}, u32[]{:S(2)}) %collective-permute-start.1) | collective-permute-done | bytes 442400 | tf_op jit(solution)/shard_map/ppermute | solution.py:30
  15.6 3.3 %collective-permute-start.7 = (bf16[432,512]{1,0:T(8,128)(2,1)S(1)}, bf16[432,512]{1,0:T(8,128)(2,1)S(1)}, u32[]{:S(2)}, u32[]{:S(2)}) collective-permute-start(bf16[432,512]{1,0:T(8,128)(2,1)S(1)} %collective-permute-done.1.refs_2_), channel_id=1, source_target_pairs={{0,14},{1,15},{2,0},{3,1},{4,2},{5,3},{6,4},{7,5},{8,6},{9,7},{10,... | collective-permute-start | bytes 1327112 | tf_op jit(solution)/shard_map/ppermute | solution.py:30
  18.9 1.8 %collective-permute-start.2 = (bf16[432,512]{1,0:T(8,128)(2,1)S(1)}, bf16[432,512]{1,0:T(8,128)(2,1)S(1)}, u32[]{:S(2)}, u32[]{:S(2)}) collective-permute-start(bf16[432,512]{1,0:T(8,128)(2,1)S(1)} %collective-permute-done.1.refs_2_), channel_id=1, source_target_pairs={{0,16},{1,17},{2,18},{3,19},{4,20},{5,21},{6,22},{7,23},{8,24},{9,... | collective-permute-start | bytes 1327112 | tf_op jit(solution)/shard_map/ppermute | solution.py:30
  21.4 5.4 %collective-permute-done.7.refs_8_ = bf16[432,512]{1,0:T(8,128)(2,1)S(1)} collective-permute-done((bf16[432,512]{1,0:T(8,128)(2,1)S(1)}, bf16[432,512]{1,0:T(8,128)(2,1)S(1)}, u32[]{:S(2)}, u32[]{:S(2)}) %collective-permute-start.7) | collective-permute-done | bytes 442400 | tf_op jit(solution)/shard_map/ppermute | solution.py:30
  26.8 2.5 %collective-permute-start.8 = (bf16[432,512]{1,0:T(8,128)(2,1)S(1)}, bf16[432,512]{1,0:T(8,128)(2,1)S(1)}, u32[]{:S(2)}, u32[]{:S(2)}) collective-permute-start(bf16[432,512]{1,0:T(8,128)(2,1)S(1)} %collective-permute-done.7.refs_8_), channel_id=1, source_target_pairs={{0,16},{1,17},{2,18},{3,19},{4,20},{5,21},{6,22},{7,23},{8,24},{9,... | collective-permute-start | bytes 1327112 | tf_op jit(solution)/shard_map/ppermute | solution.py:30
  29.3 1.3 %collective-permute-start.18 = (bf16[432,512]{1,0:T(8,128)(2,1)S(1)}, bf16[432,512]{1,0:T(8,128)(2,1)S(1)}, u32[]{:S(2)}, u32[]{:S(2)}) collective-permute-start(bf16[432,512]{1,0:T(8,128)(2,1)S(1)} %collective-permute-done.7.refs_8_), channel_id=1, source_target_pairs={{0,1},{1,0},{2,3},{3,2},{4,5},{5,4},{6,7},{7,6},{8,9},{9,8},{10,11... | collective-permute-start | bytes 1327112 | tf_op jit(solution)/shard_map/ppermute | solution.py:30
  30.7 1.0 %copy-done = bf16[512,432]{0,1:T(8,128)(2,1)S(1)} copy-done((bf16[512,432]{0,1:T(8,128)(2,1)S(1)}, bf16[512,432]{0,1:T(8,128)(2,1)}, u32[]{:S(2)}) %copy-start) | copy-done | bytes 442392
  31.7 4.7 %shard_map.28 = f32[4,2,56,2160]{3,2,1,0:T(8,128)S(1)} custom-call(bf16[432,512]{1,0:T(8,128)(2,1)S(1)} %bitcast.106, bf16[432,512]{1,0:T(8,128)(2,1)S(1)} %collective-permute-done.refs_1_, bf16[432,512]{1,0:T(8,128)(2,1)S(1)} %collective-permute-done.1.refs_2_, bf16[432,512]{1,0:T(8,128)(2,1)S(1)} %collective-permute-done.2.refs_3_, ...), custom_call_target="tpu_custom_call" | custom-call | flops 1911029760 | bytes 8388608 | tf_op jit(solution)/shard_map/pallas_call | solution.py:97
  36.7 1.4 %collective-permute-start.9 = (f16[56,2160]{1,0:T(8,128)(2,1)S(1)}, f16[56,2160]{1,0:T(8,128)(2,1)S(1)}, u32[]{:S(2)}, u32[]{:S(2)}) collective-permute-start(f16[56,2160]{1,0:T(8,128)(2,1)S(1)} %get-tuple-element.50), channel_id=1, source_target_pairs={{0,64},{1,65},{2,66},{3,67},{4,68},{5,69},{6,70},{7,71},{8,72},{9,... | collective-permute-start | bytes 725768 | tf_op jit(solution)/shard_map/ppermute | solution.py:30
  38.1 1.5 %collective-permute-start.10 = (f16[56,2160]{1,0:T(8,128)(2,1)S(1)}, f16[56,2160]{1,0:T(8,128)(2,1)S(1)}, u32[]{:S(2)}, u32[]{:S(2)}) collective-permute-start(f16[56,2160]{1,0:T(8,128)(2,1)S(1)} %get-tuple-element.49), channel_id=1, source_target_pairs={{0,192},{1,193},{2,194},{3,195},{4,196},{5,197},{6,198},{7,199},{8... | collective-permute-start | bytes 725768 | tf_op jit(solution)/shard_map/ppermute | solution.py:30
  39.6 3.5 %collective-permute-done.16.refs_4_ = bf16[432,512]{1,0:T(8,128)(2,1)S(1)} collective-permute-done((bf16[432,512]{1,0:T(8,128)(2,1)S(1)}, bf16[432,512]{1,0:T(8,128)(2,1)S(1)}, u32[]{:S(2)}, u32[]{:S(2)}) %collective-permute-start.16) | collective-permute-done | bytes 442400 | tf_op jit(solution)/shard_map/ppermute | solution.py:30
  43.9 1.4 %collective-permute-done.9 = f16[56,2160]{1,0:T(8,128)(2,1)S(1)} collective-permute-done((f16[56,2160]{1,0:T(8,128)(2,1)S(1)}, f16[56,2160]{1,0:T(8,128)(2,1)S(1)}, u32[]{:S(2)}, u32[]{:S(2)}) %collective-permute-start.9) | collective-permute-done | bytes 241952 | tf_op jit(solution)/shard_map/ppermute | solution.py:30
  46.2 1.0 collective-permute-start.11
  47.1 1.8 %collective-permute-start.12 = (f16[2,56,2160]{2,1,0:T(8,128)(2,1)S(1)}, f16[2,56,2160]{2,1,0:T(8,128)(2,1)S(1)}, u32[]{:S(2)}, u32[]{:S(2)}) collective-permute-start(f16[2,56,2160]{2,1,0:T(8,128)(2,1)S(1)} %get-tuple-element.65), channel_id=1, source_target_pairs={{0,192},{1,193},{2,194},{3,195},{4,196},{5,197},{6,198},{7,199},{8... | collective-permute-start | bytes 1451528 | tf_op jit(solution)/shard_map/ppermute | solution.py:30
  48.9 2.7 %shard_map.29 = f32[4,2,56,1296]{3,2,1,0:T(8,128)S(1)} custom-call(bf16[432,512]{1,0:T(8,128)(2,1)S(1)} %bitcast.107, bf16[432,512]{1,0:T(8,128)(2,1)S(1)} %collective-permute-done.refs_1_, bf16[432,512]{1,0:T(8,128)(2,1)S(1)} %collective-permute-done.3.refs_4_.refs_2_, bf16[432,512]{1,0:T(8,128)(2,1)S(1)} %collective-permute-done.4.refs_5_.refs_3_, ...), custom_call_target="tpu_custom_call" | custom-call | flops 1146617856 | bytes 8388608 | tf_op jit(solution)/shard_map/pallas_call | solution.py:97
  52.0 2.7 %collective-permute-start.21 = (f16[56,1296]{1,0:T(8,128)(2,1)S(1)}, f16[56,1296]{1,0:T(8,128)(2,1)S(1)}, u32[]{:S(2)}, u32[]{:S(2)}) collective-permute-start(f16[56,1296]{1,0:T(8,128)(2,1)S(1)} %get-tuple-element.55), channel_id=1, source_target_pairs={{255,191},{254,190},{253,189},{252,188},{251,187},{250,186},{249,1... | collective-permute-start | bytes 435464 | tf_op jit(solution)/shard_map/ppermute | solution.py:30
  54.7 7.7 %collective-permute-done.20 = f16[56,1296]{1,0:T(8,128)(2,1)S(1)} collective-permute-done((f16[56,1296]{1,0:T(8,128)(2,1)S(1)}, f16[56,1296]{1,0:T(8,128)(2,1)S(1)}, u32[]{:S(2)}, u32[]{:S(2)}) %collective-permute-start.20) | collective-permute-done | bytes 145184 | tf_op jit(solution)/shard_map/ppermute | solution.py:30
  63.4 2.6 %collective-permute-start.23 = (f16[2,56,1296]{2,1,0:T(8,128)(2,1)S(1)}, f16[2,56,1296]{2,1,0:T(8,128)(2,1)S(1)}, u32[]{:S(2)}, u32[]{:S(2)}) collective-permute-start(f16[2,56,1296]{2,1,0:T(8,128)(2,1)S(1)} %get-tuple-element.63), channel_id=1, source_target_pairs={{255,191},{254,190},{253,189},{252,188},{251,187},{250,186},{249,1... | collective-permute-start | bytes 870920 | tf_op jit(solution)/shard_map/ppermute | solution.py:30
  67.0 2.8 %collective-permute-start.13 = (f16[56,2160]{1,0:T(8,128)(2,1)S(1)}, f16[56,2160]{1,0:T(8,128)(2,1)S(1)}, u32[]{:S(2)}, u32[]{:S(2)}) collective-permute-start(f16[56,2160]{1,0:T(8,128)(2,1)S(1)} %fusion.10), channel_id=1, source_target_pairs={{0,32},{1,33},{2,34},{3,35},{4,36},{5,37},{6,38},{7,39},{8,40},{9,... | collective-permute-start | bytes 725768 | tf_op jit(solution)/shard_map/ppermute | solution.py:30
  69.8 1.6 %collective-permute-done.22 = f16[2,56,1296]{2,1,0:T(8,128)(2,1)S(1)} collective-permute-done((f16[2,56,1296]{2,1,0:T(8,128)(2,1)S(1)}, f16[2,56,1296]{2,1,0:T(8,128)(2,1)S(1)}, u32[]{:S(2)}, u32[]{:S(2)}) %collective-permute-start.22) | collective-permute-done | bytes 290336 | tf_op jit(solution)/shard_map/ppermute | solution.py:30
  73.2 2.8 %collective-permute-start.25 = (f16[56,432]{1,0:T(8,128)(2,1)S(1)}, f16[56,432]{1,0:T(8,128)(2,1)S(1)}, u32[]{:S(2)}, u32[]{:S(2)}) collective-permute-start(f16[56,432]{1,0:T(8,128)(2,1)S(1)} %slice.237), channel_id=1, source_target_pairs={{0,46},{1,47},{2,32},{3,33},{4,34},{5,35},{6,36},{7,37},{8,38},{9,... | collective-permute-start | bytes 145160 | tf_op jit(solution)/shard_map/ppermute | solution.py:30
  76.0 1.1 %collective-permute-start.26 = (f16[56,864]{1,0:T(8,128)(2,1)S(1)}, f16[56,864]{1,0:T(8,128)(2,1)S(1)}, u32[]{:S(2)}, u32[]{:S(2)}) collective-permute-start(f16[56,864]{1,0:T(8,128)(2,1)S(1)} %slice.238), channel_id=1, source_target_pairs={{0,12},{1,13},{2,14},{3,15},{4,0},{5,1},{6,2},{7,3},{8,4},{9,5},{1... | collective-permute-start | bytes 290312 | tf_op jit(solution)/shard_map/ppermute | solution.py:30
  77.1 1.1 %collective-permute-start.27 = (f16[56,864]{1,0:T(8,128)(2,1)S(1)}, f16[56,864]{1,0:T(8,128)(2,1)S(1)}, u32[]{:S(2)}, u32[]{:S(2)}) collective-permute-start(f16[56,864]{1,0:T(8,128)(2,1)S(1)} %slice.239), channel_id=1, source_target_pairs={{0,44},{1,45},{2,46},{3,47},{4,32},{5,33},{6,34},{7,35},{8,36},{9,... | collective-permute-start | bytes 290312 | tf_op jit(solution)/shard_map/ppermute | solution.py:30
  78.7 1.3 %collective-permute-start.14 = (f32[56,432]{1,0:T(8,128)S(1)}, f32[56,432]{1,0:T(8,128)S(1)}, u32[]{:S(2)}, u32[]{:S(2)}) collective-permute-start(f32[56,432]{1,0:T(8,128)S(1)} %get-tuple-element.61), channel_id=1, source_target_pairs={{0,1},{1,0},{2,3},{3,2},{4,5},{5,4},{6,7},{7,6},{8,9},{9,8},{10,11... | collective-permute-start | bytes 290312 | tf_op jit(solution)/shard_map/ppermute | solution.py:30
  80.0 3.5 %collective-permute-start.15 = (f32[56,864]{1,0:T(8,128)S(1)}, f32[56,864]{1,0:T(8,128)S(1)}, u32[]{:S(2)}, u32[]{:S(2)}) collective-permute-start(f32[56,864]{1,0:T(8,128)S(1)} %slice.226), channel_id=1, source_target_pairs={{0,14},{1,15},{2,0},{3,1},{4,2},{5,3},{6,4},{7,5},{8,6},{9,7},{10,... | collective-permute-start | bytes 580616 | tf_op jit(solution)/shard_map/ppermute | solution.py:30
  83.5 2.1 %collective-permute-done.27 = f16[56,864]{1,0:T(8,128)(2,1)S(1)} collective-permute-done((f16[56,864]{1,0:T(8,128)(2,1)S(1)}, f16[56,864]{1,0:T(8,128)(2,1)S(1)}, u32[]{:S(2)}, u32[]{:S(2)}) %collective-permute-start.27) | collective-permute-done | bytes 96800 | tf_op jit(solution)/shard_map/ppermute | solution.py:30
  85.9 3.0 %collective-permute-done.15 = f32[56,864]{1,0:T(8,128)S(1)} collective-permute-done((f32[56,864]{1,0:T(8,128)S(1)}, f32[56,864]{1,0:T(8,128)S(1)}, u32[]{:S(2)}, u32[]{:S(2)}) %collective-permute-start.15) | collective-permute-done | bytes 193568 | tf_op jit(solution)/shard_map/ppermute | solution.py:30
  89.4 5.8 %collective-permute-start.28 = (f32[27,3456]{1,0:T(8,128)S(1)}, f32[27,3456]{1,0:T(8,128)S(1)}, u32[]{:S(2)}, u32[]{:S(2)}) collective-permute-start(f32[27,3456]{1,0:T(8,128)S(1)} %constant_dynamic-slice_fusion.3), channel_id=1, source_target_pairs={{0,16},{1,17},{2,18},{3,19},{4,20},{5,21},{6,22},{7,23},{8,24},{9,... | collective-permute-start | bytes 1119752 | tf_op jit(solution)/shard_map/ppermute | solution.py:30
  95.2 1.4 %collective-permute-done.28.theirs = f32[27,3456]{1,0:T(8,128)S(1)} collective-permute-done((f32[27,3456]{1,0:T(8,128)S(1)}, f32[27,3456]{1,0:T(8,128)S(1)}, u32[]{:S(2)}, u32[]{:S(2)}) %collective-permute-start.28) | collective-permute-done | bytes 373280 | tf_op jit(solution)/shard_map/ppermute | solution.py:30
  96.6 1.6 %shard_map.30 = f32[27,6912]{1,0:T(8,128)} custom-call(f32[56,3456]{1,0:T(8,128)S(1)} %concatenate.3.mine, f32[27,3456]{1,0:T(8,128)S(1)} %collective-permute-done.28.theirs, f32[27,6912]{1,0:T(8,128)S(1)} %copy-done.1), custom_call_target="tpu_custom_call" | custom-call | bytes 4194304 | tf_op jit(solution)/shard_map/pallas_call | solution.py:202
  (98 shorter events, 8.7 us)
Async XLA Ops:
  0.0 15.6 %collective-permute-start.1 = (bf16[432,512]{1,0:T(8,128)(2,1)}, bf16[432,512]{1,0:T(8,128)(2,1)S(1)}, u32[]{:S(2)}, u32[]{:S(2)}) collective-permute-start(bf16[432,512]{1,0:T(8,128)(2,1)} %bitcast.102), channel_id=1, source_target_pairs={{0,14},{1,15},{2,0},{3,1},{4,2},{5,3},{6,4},{7,5},{8,6},{9,7},{10,... | collective-permute-start | bytes 1327112 | tf_op jit(solution)/shard_map/ppermute | solution.py:30
  6.4 12.5 %collective-permute-start = (bf16[432,512]{1,0:T(8,128)(2,1)}, bf16[432,512]{1,0:T(8,128)(2,1)S(1)}, u32[]{:S(2)}, u32[]{:S(2)}) collective-permute-start(bf16[432,512]{1,0:T(8,128)(2,1)} %bitcast.103), channel_id=1, source_target_pairs={{0,16},{1,17},{2,18},{3,19},{4,20},{5,21},{6,22},{7,23},{8,24},{9,... | collective-permute-start | bytes 1327112 | tf_op jit(solution)/shard_map/ppermute | solution.py:30
  7.4 13.3 %collective-permute-start.3 = (bf16[432,512]{1,0:T(8,128)(2,1)}, bf16[432,512]{1,0:T(8,128)(2,1)S(1)}, u32[]{:S(2)}, u32[]{:S(2)}) collective-permute-start(bf16[432,512]{1,0:T(8,128)(2,1)} %bitcast.104), channel_id=1, source_target_pairs={{0,2},{1,3},{2,4},{3,5},{4,6},{5,7},{6,8},{7,9},{8,10},{9,11},{10,... | collective-permute-start | bytes 1327112 | tf_op jit(solution)/shard_map/ppermute | solution.py:30
  7.4 14.0 %collective-permute-start.5 = (bf16[432,512]{1,0:T(8,128)(2,1)}, bf16[432,512]{1,0:T(8,128)(2,1)S(1)}, u32[]{:S(2)}, u32[]{:S(2)}) collective-permute-start(bf16[432,512]{1,0:T(8,128)(2,1)} %bitcast.105), channel_id=1, source_target_pairs={{0,1},{1,0},{2,3},{3,2},{4,5},{5,4},{6,7},{7,6},{8,9},{9,8},{10,11... | collective-permute-start | bytes 1327112 | tf_op jit(solution)/shard_map/ppermute | solution.py:30
  15.6 11.2 %collective-permute-start.7 = (bf16[432,512]{1,0:T(8,128)(2,1)S(1)}, bf16[432,512]{1,0:T(8,128)(2,1)S(1)}, u32[]{:S(2)}, u32[]{:S(2)}) collective-permute-start(bf16[432,512]{1,0:T(8,128)(2,1)S(1)} %collective-permute-done.1.refs_2_), channel_id=1, source_target_pairs={{0,14},{1,15},{2,0},{3,1},{4,2},{5,3},{6,4},{7,5},{8,6},{9,7},{10,... | collective-permute-start | bytes 1327112 | tf_op jit(solution)/shard_map/ppermute | solution.py:30
  18.9 10.4 %collective-permute-start.2 = (bf16[432,512]{1,0:T(8,128)(2,1)S(1)}, bf16[432,512]{1,0:T(8,128)(2,1)S(1)}, u32[]{:S(2)}, u32[]{:S(2)}) collective-permute-start(bf16[432,512]{1,0:T(8,128)(2,1)S(1)} %collective-permute-done.1.refs_2_), channel_id=1, source_target_pairs={{0,16},{1,17},{2,18},{3,19},{4,20},{5,21},{6,22},{7,23},{8,24},{9,... | collective-permute-start | bytes 1327112 | tf_op jit(solution)/shard_map/ppermute | solution.py:30
  20.7 9.9 %collective-permute-start.4 = (bf16[432,512]{1,0:T(8,128)(2,1)S(1)}, bf16[432,512]{1,0:T(8,128)(2,1)S(1)}, u32[]{:S(2)}, u32[]{:S(2)}) collective-permute-start(bf16[432,512]{1,0:T(8,128)(2,1)S(1)} %collective-permute-done.3.refs_4_.refs_2_), channel_id=1, source_target_pairs={{0,16},{1,17},{2,18},{3,19},{4,20},{5,21},{6,22},{7,23},{8,24},{9,... | collective-permute-start | bytes 1327112 | tf_op jit(solution)/shard_map/ppermute | solution.py:30
  21.4 9.2 %collective-permute-start.6 = (bf16[432,512]{1,0:T(8,128)(2,1)S(1)}, bf16[432,512]{1,0:T(8,128)(2,1)}, u32[]{:S(2)}, u32[]{:S(2)}) collective-permute-start(bf16[432,512]{1,0:T(8,128)(2,1)S(1)} %collective-permute-done.5.refs_6_), channel_id=1, source_target_pairs={{0,16},{1,17},{2,18},{3,19},{4,20},{5,21},{6,22},{7,23},{8,24},{9,... | collective-permute-start | bytes 1327112 | tf_op jit(solution)/shard_map/ppermute | solution.py:30
  26.8 3.9 %collective-permute-start.8 = (bf16[432,512]{1,0:T(8,128)(2,1)S(1)}, bf16[432,512]{1,0:T(8,128)(2,1)S(1)}, u32[]{:S(2)}, u32[]{:S(2)}) collective-permute-start(bf16[432,512]{1,0:T(8,128)(2,1)S(1)} %collective-permute-done.7.refs_8_), channel_id=1, source_target_pairs={{0,16},{1,17},{2,18},{3,19},{4,20},{5,21},{6,22},{7,23},{8,24},{9,... | collective-permute-start | bytes 1327112 | tf_op jit(solution)/shard_map/ppermute | solution.py:30
  29.3 13.9 %collective-permute-start.16 = (bf16[432,512]{1,0:T(8,128)(2,1)S(1)}, bf16[432,512]{1,0:T(8,128)(2,1)S(1)}, u32[]{:S(2)}, u32[]{:S(2)}) collective-permute-start(bf16[432,512]{1,0:T(8,128)(2,1)S(1)} %collective-permute-done.3.refs_4_.refs_2_), channel_id=1, source_target_pairs={{0,2},{1,3},{2,4},{3,5},{4,6},{5,7},{6,8},{7,9},{8,10},{9,11},{10,... | collective-permute-start | bytes 1327112 | tf_op jit(solution)/shard_map/ppermute | solution.py:30
  29.3 14.5 %collective-permute-start.18 = (bf16[432,512]{1,0:T(8,128)(2,1)S(1)}, bf16[432,512]{1,0:T(8,128)(2,1)S(1)}, u32[]{:S(2)}, u32[]{:S(2)}) collective-permute-start(bf16[432,512]{1,0:T(8,128)(2,1)S(1)} %collective-permute-done.7.refs_8_), channel_id=1, source_target_pairs={{0,1},{1,0},{2,3},{3,2},{4,5},{5,4},{6,7},{7,6},{8,9},{9,8},{10,11... | collective-permute-start | bytes 1327112 | tf_op jit(solution)/shard_map/ppermute | solution.py:30
  30.7 1.0 %copy-start = (bf16[512,432]{0,1:T(8,128)(2,1)S(1)}, bf16[512,432]{0,1:T(8,128)(2,1)}, u32[]{:S(2)}) copy-start(bf16[512,432]{0,1:T(8,128)(2,1)} %param.2) | copy-start | bytes 1327108
  36.7 8.6 %collective-permute-start.9 = (f16[56,2160]{1,0:T(8,128)(2,1)S(1)}, f16[56,2160]{1,0:T(8,128)(2,1)S(1)}, u32[]{:S(2)}, u32[]{:S(2)}) collective-permute-start(f16[56,2160]{1,0:T(8,128)(2,1)S(1)} %get-tuple-element.50), channel_id=1, source_target_pairs={{0,64},{1,65},{2,66},{3,67},{4,68},{5,69},{6,70},{7,71},{8,72},{9,... | collective-permute-start | bytes 725768 | tf_op jit(solution)/shard_map/ppermute | solution.py:30
  38.1 7.2 %collective-permute-start.10 = (f16[56,2160]{1,0:T(8,128)(2,1)S(1)}, f16[56,2160]{1,0:T(8,128)(2,1)S(1)}, u32[]{:S(2)}, u32[]{:S(2)}) collective-permute-start(f16[56,2160]{1,0:T(8,128)(2,1)S(1)} %get-tuple-element.49), channel_id=1, source_target_pairs={{0,192},{1,193},{2,194},{3,195},{4,196},{5,197},{6,198},{7,199},{8... | collective-permute-start | bytes 725768 | tf_op jit(solution)/shard_map/ppermute | solution.py:30
  43.1 5.8 %collective-permute-start.17 = (bf16[432,512]{1,0:T(8,128)(2,1)S(1)}, bf16[432,512]{1,0:T(8,128)(2,1)S(1)}, u32[]{:S(2)}, u32[]{:S(2)}) collective-permute-start(bf16[432,512]{1,0:T(8,128)(2,1)S(1)} %collective-permute-done.16.refs_4_), channel_id=1, source_target_pairs={{0,16},{1,17},{2,18},{3,19},{4,20},{5,21},{6,22},{7,23},{8,24},{9,... | collective-permute-start | bytes 1327112 | tf_op jit(solution)/shard_map/ppermute | solution.py:30
  43.8 5.2 %collective-permute-start.19 = (bf16[432,512]{1,0:T(8,128)(2,1)S(1)}, bf16[432,512]{1,0:T(8,128)(2,1)S(1)}, u32[]{:S(2)}, u32[]{:S(2)}) collective-permute-start(bf16[432,512]{1,0:T(8,128)(2,1)S(1)} %collective-permute-done.18.refs_6_), channel_id=1, source_target_pairs={{0,16},{1,17},{2,18},{3,19},{4,20},{5,21},{6,22},{7,23},{8,24},{9,... | collective-permute-start | bytes 1327112 | tf_op jit(solution)/shard_map/ppermute | solution.py:30
  46.2 19.9 %collective-permute-start.11 = (f16[2,56,2160]{2,1,0:T(8,128)(2,1)S(1)}, f16[2,56,2160]{2,1,0:T(8,128)(2,1)S(1)}, u32[]{:S(2)}, u32[]{:S(2)}) collective-permute-start(f16[2,56,2160]{2,1,0:T(8,128)(2,1)S(1)} %get-tuple-element.66), channel_id=1, source_target_pairs={{0,64},{1,65},{2,66},{3,67},{4,68},{5,69},{6,70},{7,71},{8,72},{9,... | collective-permute-start | bytes 1451528 | tf_op jit(solution)/shard_map/ppermute | solution.py:30
  47.1 18.9 %collective-permute-start.12 = (f16[2,56,2160]{2,1,0:T(8,128)(2,1)S(1)}, f16[2,56,2160]{2,1,0:T(8,128)(2,1)S(1)}, u32[]{:S(2)}, u32[]{:S(2)}) collective-permute-start(f16[2,56,2160]{2,1,0:T(8,128)(2,1)S(1)} %get-tuple-element.65), channel_id=1, source_target_pairs={{0,192},{1,193},{2,194},{3,195},{4,196},{5,197},{6,198},{7,199},{8... | collective-permute-start | bytes 1451528 | tf_op jit(solution)/shard_map/ppermute | solution.py:30
  51.9 10.5 %collective-permute-start.20 = (f16[56,1296]{1,0:T(8,128)(2,1)S(1)}, f16[56,1296]{1,0:T(8,128)(2,1)S(1)}, u32[]{:S(2)}, u32[]{:S(2)}) collective-permute-start(f16[56,1296]{1,0:T(8,128)(2,1)S(1)} %get-tuple-element.56), channel_id=1, source_target_pairs={{255,63},{254,62},{253,61},{252,60},{251,59},{250,58},{249,57},{24... | collective-permute-start | bytes 435464 | tf_op jit(solution)/shard_map/ppermute | solution.py:30
  52.0 10.4 %collective-permute-start.21 = (f16[56,1296]{1,0:T(8,128)(2,1)S(1)}, f16[56,1296]{1,0:T(8,128)(2,1)S(1)}, u32[]{:S(2)}, u32[]{:S(2)}) collective-permute-start(f16[56,1296]{1,0:T(8,128)(2,1)S(1)} %get-tuple-element.55), channel_id=1, source_target_pairs={{255,191},{254,190},{253,189},{252,188},{251,187},{250,186},{249,1... | collective-permute-start | bytes 435464 | tf_op jit(solution)/shard_map/ppermute | solution.py:30
  63.1 8.4 %collective-permute-start.22 = (f16[2,56,1296]{2,1,0:T(8,128)(2,1)S(1)}, f16[2,56,1296]{2,1,0:T(8,128)(2,1)S(1)}, u32[]{:S(2)}, u32[]{:S(2)}) collective-permute-start(f16[2,56,1296]{2,1,0:T(8,128)(2,1)S(1)} %get-tuple-element.64), channel_id=1, source_target_pairs={{255,63},{254,62},{253,61},{252,60},{251,59},{250,58},{249,57},{24... | collective-permute-start | bytes 870920 | tf_op jit(solution)/shard_map/ppermute | solution.py:30
  63.4 8.0 %collective-permute-start.23 = (f16[2,56,1296]{2,1,0:T(8,128)(2,1)S(1)}, f16[2,56,1296]{2,1,0:T(8,128)(2,1)S(1)}, u32[]{:S(2)}, u32[]{:S(2)}) collective-permute-start(f16[2,56,1296]{2,1,0:T(8,128)(2,1)S(1)} %get-tuple-element.63), channel_id=1, source_target_pairs={{255,191},{254,190},{253,189},{252,188},{251,187},{250,186},{249,1... | collective-permute-start | bytes 870920 | tf_op jit(solution)/shard_map/ppermute | solution.py:30
  67.0 11.2 %collective-permute-start.13 = (f16[56,2160]{1,0:T(8,128)(2,1)S(1)}, f16[56,2160]{1,0:T(8,128)(2,1)S(1)}, u32[]{:S(2)}, u32[]{:S(2)}) collective-permute-start(f16[56,2160]{1,0:T(8,128)(2,1)S(1)} %fusion.10), channel_id=1, source_target_pairs={{0,32},{1,33},{2,34},{3,35},{4,36},{5,37},{6,38},{7,39},{8,40},{9,... | collective-permute-start | bytes 725768 | tf_op jit(solution)/shard_map/ppermute | solution.py:30
  72.3 24.3 %copy-start.1 = (f32[27,6912]{1,0:T(8,128)S(1)}, f32[27,6912]{1,0:T(8,128)}, u32[]{:S(2)}) copy-start(f32[27,6912]{1,0:T(8,128)} %previous.1) | copy-start | bytes 2239492
  72.5 7.5 %collective-permute-start.24 = (f16[56,432]{1,0:T(8,128)(2,1)S(1)}, f16[56,432]{1,0:T(8,128)(2,1)S(1)}, u32[]{:S(2)}, u32[]{:S(2)}) collective-permute-start(f16[56,432]{1,0:T(8,128)(2,1)S(1)} %slice.236), channel_id=1, source_target_pairs={{0,14},{1,15},{2,0},{3,1},{4,2},{5,3},{6,4},{7,5},{8,6},{9,7},{10,... | collective-permute-start | bytes 145160 | tf_op jit(solution)/shard_map/ppermute | solution.py:30
  73.2 10.3 %collective-permute-start.25 = (f16[56,432]{1,0:T(8,128)(2,1)S(1)}, f16[56,432]{1,0:T(8,128)(2,1)S(1)}, u32[]{:S(2)}, u32[]{:S(2)}) collective-permute-start(f16[56,432]{1,0:T(8,128)(2,1)S(1)} %slice.237), channel_id=1, source_target_pairs={{0,46},{1,47},{2,32},{3,33},{4,34},{5,35},{6,36},{7,37},{8,38},{9,... | collective-permute-start | bytes 145160 | tf_op jit(solution)/shard_map/ppermute | solution.py:30
  76.0 7.4 %collective-permute-start.26 = (f16[56,864]{1,0:T(8,128)(2,1)S(1)}, f16[56,864]{1,0:T(8,128)(2,1)S(1)}, u32[]{:S(2)}, u32[]{:S(2)}) collective-permute-start(f16[56,864]{1,0:T(8,128)(2,1)S(1)} %slice.238), channel_id=1, source_target_pairs={{0,12},{1,13},{2,14},{3,15},{4,0},{5,1},{6,2},{7,3},{8,4},{9,5},{1... | collective-permute-start | bytes 290312 | tf_op jit(solution)/shard_map/ppermute | solution.py:30
  77.1 8.4 %collective-permute-start.27 = (f16[56,864]{1,0:T(8,128)(2,1)S(1)}, f16[56,864]{1,0:T(8,128)(2,1)S(1)}, u32[]{:S(2)}, u32[]{:S(2)}) collective-permute-start(f16[56,864]{1,0:T(8,128)(2,1)S(1)} %slice.239), channel_id=1, source_target_pairs={{0,44},{1,45},{2,46},{3,47},{4,32},{5,33},{6,34},{7,35},{8,36},{9,... | collective-permute-start | bytes 290312 | tf_op jit(solution)/shard_map/ppermute | solution.py:30
  78.7 7.2 %collective-permute-start.14 = (f32[56,432]{1,0:T(8,128)S(1)}, f32[56,432]{1,0:T(8,128)S(1)}, u32[]{:S(2)}, u32[]{:S(2)}) collective-permute-start(f32[56,432]{1,0:T(8,128)S(1)} %get-tuple-element.61), channel_id=1, source_target_pairs={{0,1},{1,0},{2,3},{3,2},{4,5},{5,4},{6,7},{7,6},{8,9},{9,8},{10,11... | collective-permute-start | bytes 290312 | tf_op jit(solution)/shard_map/ppermute | solution.py:30
  80.0 9.0 %collective-permute-start.15 = (f32[56,864]{1,0:T(8,128)S(1)}, f32[56,864]{1,0:T(8,128)S(1)}, u32[]{:S(2)}, u32[]{:S(2)}) collective-permute-start(f32[56,864]{1,0:T(8,128)S(1)} %slice.226), channel_id=1, source_target_pairs={{0,14},{1,15},{2,0},{3,1},{4,2},{5,3},{6,4},{7,5},{8,6},{9,7},{10,... | collective-permute-start | bytes 580616 | tf_op jit(solution)/shard_map/ppermute | solution.py:30
  89.4 7.2 %collective-permute-start.28 = (f32[27,3456]{1,0:T(8,128)S(1)}, f32[27,3456]{1,0:T(8,128)S(1)}, u32[]{:S(2)}, u32[]{:S(2)}) collective-permute-start(f32[27,3456]{1,0:T(8,128)S(1)} %constant_dynamic-slice_fusion.3), channel_id=1, source_target_pairs={{0,16},{1,17},{2,18},{3,19},{4,20},{5,21},{6,22},{7,23},{8,24},{9,... | collective-permute-start | bytes 1119752 | tf_op jit(solution)/shard_map/ppermute | solution.py:30
where the time goes:
time: 98.3 us; the launch traced here: 98.1 us
  starting transfers between devices  49.3 us (50%)
  waiting for transfers between devices  33.3 us (34%)
  Pallas kernels  8.96 us (9%)
  other arithmetic  4.06 us (4%)
  local copies, waits for them, and re-layouts  2.09 us (2%)
    ppermute x29, starting transfers between devices, move(): return lax.ppermute(value, AXES, pairs[::-1] if turned else pairs)  49.3 us
    ppermute x29, waiting for transfers between devices, move(): return lax.ppermute(value, AXES, pairs[::-1] if turned else pairs)  33.3 us
    pallas_call x2, Pallas kernels, products(): pl.pallas_call(functools.partial(products_kernel, units, len(shards), wid...  7.4 us
  transfers between devices with their start and end apart: 29, of which 10 were waited for; matrix products, arithmetic and copies ran while one was open for 5% of the time, Pallas kernels for 8%

commit v1 on v0

--- a/solution.py
+++ b/solution.py
@@ -165,7 +165,7 @@
 
 
 def x_last(summed, arrived, n_rows, xh_at):
-    return chunk_of(summed, xh_at) + unpacked(arrived, n_rows)
+    return added(chunk_of(summed, xh_at), unpacked(arrived, n_rows), n_rows)
 
 
 HELD = (
@@ -257,13 +257,15 @@
 
     w = width
     got_a = shifted(sum1[:, w : 2 * w], (0, 1), (1, 0))
-    got_b = shifted(sum1[:, 2 * w : 4 * w], (-1, 0), (2, 0))
     summed2 = y_last(part2, got2, rows, y_at)
     keep, give = chunk_of(summed2, xh_at), packed(chunk_of(summed2, xh_at + 1), rows)
     kept = packed(keep, rows)
-    d_same, d_other = shifted(kept[:, :w], (-1, 0), None), shifted(give[:, :w], (-1, 0), (0, 0), 1)
+    joined = jnp.concatenate([packed(sum1[:, 2 * w : 4 * w], rows), kept[:, :w]], axis=1)
+    joined = shifted(joined, (-1, 0), (2, 0))
+    d_other = shifted(give[:, :w], (-1, 0), (0, 0), 1)
     e_same, e_other = shifted(kept[:, w:], (-2, 0), (2, 1)), shifted(give[:, w:], (-2, 0), (2, 1), 1)
-    d_same, d_other, e_same, e_other = lax.optimization_barrier((d_same, d_other, e_same, e_other))
+    joined, d_other, e_same, e_other = lax.optimization_barrier((joined, d_other, e_same, e_other))
+    got_b, d_same = unpacked(joined[:, : 2 * w], rows), joined[:, 2 * w :]
     got_d = jnp.where(c_at == 0, unpacked(d_same, rows), keep[:, :w]) + unpacked(d_other, rows)
     got_e = unpacked(e_same, rows) + unpacked(e_other, rows)
     mine = jnp.concatenate([sum1[:, :w], got_a, got_b, sum1[:, 4 * w :], got_d, got_e], axis=1)

time: 98.3 us -> 96.2 us (0.979)
  starting transfers between devices: 49.3 us -> 45.4 us
  waiting for transfers between devices: 33.3 us -> 34.6 us
    ppermute x29 -> x28, starting transfers between devices: 49.3 us -> 45.4 us  [move(): return lax.ppermute(value, AXES, pairs[::-1] if turned else pairs)]
    ppermute x29 -> x28, waiting for transfers between devices: 33.3 us -> 34.6 us  [move(): return lax.ppermute(value, AXES, pairs[::-1] if turned else pairs)]
  transfers between devices with their start and end apart: 29 -> 28, of which waited for: 10 -> 13; matrix products, arithmetic and copies ran while one was open for 5% -> 5% of each run, Pallas kernels for 8% -> 8%
where the time goes in v1:
time: 96.2 us; the launch traced here: 96.1 us
  starting transfers between devices  45.4 us (47%)
  waiting for transfers between devices  34.6 us (36%)
  Pallas kernels  8.95 us (9%)
  other arithmetic  4.64 us (5%)
  local copies, waits for them, and re-layouts  1.97 us (2%)
    ppermute x28, starting transfers between devices, move(): return lax.ppermute(value, AXES, pairs[::-1] if turned else pairs)  45.4 us
    ppermute x28, waiting for transfers between devices, move(): return lax.ppermute(value, AXES, pairs[::-1] if turned else pairs)  34.6 us
    pallas_call x2, Pallas kernels, products(): pl.pallas_call(functools.partial(products_kernel, units, len(shards), wid...  7.4 us
  transfers between devices with their start and end apart: 28, of which 13 were waited for; matrix products, arithmetic and copies ran while one was open for 5% of the time, Pallas kernels for 8%

profile of v1, /device:TPU:1, one launch (start us, length us, event | category | flops | bytes accessed | tf_op | source)
XLA Modules:
  0.0 96.1 jit_solution(8998961879800418366)
XLA Ops:
  0.0 6.4 %collective-permute-start.1 = (bf16[432,512]{1,0:T(8,128)(2,1)}, bf16[432,512]{1,0:T(8,128)(2,1)S(1)}, u32[]{:S(2)}, u32[]{:S(2)}) collective-permute-start(bf16[432,512]{1,0:T(8,128)(2,1)} %bitcast.109), channel_id=1, source_target_pairs={{0,14},{1,15},{2,0},{3,1},{4,2},{5,3},{6,4},{7,5},{8,6},{9,7},{10,... | collective-permute-start | bytes 1327112 | tf_op jit(solution)/shard_map/ppermute | solution.py:30
  6.4 1.0 collective-permute-start
  7.4 1.2 %collective-permute-start.5 = (bf16[432,512]{1,0:T(8,128)(2,1)}, bf16[432,512]{1,0:T(8,128)(2,1)S(1)}, u32[]{:S(2)}, u32[]{:S(2)}) collective-permute-start(bf16[432,512]{1,0:T(8,128)(2,1)} %bitcast.112), channel_id=1, source_target_pairs={{0,1},{1,0},{2,3},{3,2},{4,5},{5,4},{6,7},{7,6},{8,9},{9,8},{10,11... | collective-permute-start | bytes 1327112 | tf_op jit(solution)/shard_map/ppermute | solution.py:30
  8.6 7.0 %collective-permute-done.1.refs_2_ = bf16[432,512]{1,0:T(8,128)(2,1)S(1)} collective-permute-done((bf16[432,512]{1,0:T(8,128)(2,1)}, bf16[432,512]{1,0:T(8,128)(2,1)S(1)}, u32[]{:S(2)}, u32[]{:S(2)}) %collective-permute-start.1) | collective-permute-done | bytes 442400 | tf_op jit(solution)/shard_map/ppermute | solution.py:30
  15.6 3.3 %collective-permute-start.7 = (bf16[432,512]{1,0:T(8,128)(2,1)S(1)}, bf16[432,512]{1,0:T(8,128)(2,1)S(1)}, u32[]{:S(2)}, u32[]{:S(2)}) collective-permute-start(bf16[432,512]{1,0:T(8,128)(2,1)S(1)} %collective-permute-done.1.refs_2_), channel_id=1, source_target_pairs={{0,14},{1,15},{2,0},{3,1},{4,2},{5,3},{6,4},{7,5},{8,6},{9,7},{10,... | collective-permute-start | bytes 1327112 | tf_op jit(solution)/shard_map/ppermute | solution.py:30
  18.9 1.7 %collective-permute-done.3.refs_4_.refs_2_ = bf16[432,512]{1,0:T(8,128)(2,1)S(1)} collective-permute-done((bf16[432,512]{1,0:T(8,128)(2,1)}, bf16[432,512]{1,0:T(8,128)(2,1)S(1)}, u32[]{:S(2)}, u32[]{:S(2)}) %collective-permute-start.3) | collective-permute-done | bytes 442400 | tf_op jit(solution)/shard_map/ppermute | solution.py:30
  20.6 0.8 collective-permute-start.4
  21.9 4.9 %collective-permute-done.7.refs_8_ = bf16[432,512]{1,0:T(8,128)(2,1)S(1)} collective-permute-done((bf16[432,512]{1,0:T(8,128)(2,1)S(1)}, bf16[432,512]{1,0:T(8,128)(2,1)S(1)}, u32[]{:S(2)}, u32[]{:S(2)}) %collective-permute-start.7) | collective-permute-done | bytes 442400 | tf_op jit(solution)/shard_map/ppermute | solution.py:30
  26.8 2.5 %collective-permute-start.8 = (bf16[432,512]{1,0:T(8,128)(2,1)S(1)}, bf16[432,512]{1,0:T(8,128)(2,1)S(1)}, u32[]{:S(2)}, u32[]{:S(2)}) collective-permute-start(bf16[432,512]{1,0:T(8,128)(2,1)S(1)} %collective-permute-done.7.refs_8_), channel_id=1, source_target_pairs={{0,16},{1,17},{2,18},{3,19},{4,20},{5,21},{6,22},{7,23},{8,24},{9,... | collective-permute-start | bytes 1327112 | tf_op jit(solution)/shard_map/ppermute | solution.py:30
  29.3 1.3 %collective-permute-start.17 = (bf16[432,512]{1,0:T(8,128)(2,1)S(1)}, bf16[432,512]{1,0:T(8,128)(2,1)S(1)}, u32[]{:S(2)}, u32[]{:S(2)}) collective-permute-start(bf16[432,512]{1,0:T(8,128)(2,1)S(1)} %collective-permute-done.7.refs_8_), channel_id=1, source_target_pairs={{0,1},{1,0},{2,3},{3,2},{4,5},{5,4},{6,7},{7,6},{8,9},{9,8},{10,11... | collective-permute-start | bytes 1327112 | tf_op jit(solution)/shard_map/ppermute | solution.py:30
  30.7 1.0 %copy-done = bf16[512,432]{0,1:T(8,128)(2,1)S(1)} copy-done((bf16[512,432]{0,1:T(8,128)(2,1)S(1)}, bf16[512,432]{0,1:T(8,128)(2,1)}, u32[]{:S(2)}) %copy-start) | copy-done | bytes 442392
  31.7 4.7 %shard_map.28 = f32[4,2,56,2160]{3,2,1,0:T(8,128)S(1)} custom-call(bf16[432,512]{1,0:T(8,128)(2,1)S(1)} %bitcast.113, bf16[432,512]{1,0:T(8,128)(2,1)S(1)} %collective-permute-done.refs_1_, bf16[432,512]{1,0:T(8,128)(2,1)S(1)} %collective-permute-done.1.refs_2_, bf16[432,512]{1,0:T(8,128)(2,1)S(1)} %collective-permute-done.2.refs_3_, ...), custom_call_target="tpu_custom_call" | custom-call | flops 1911029760 | bytes 8388608 | tf_op jit(solution)/shard_map/pallas_call | solution.py:97
  36.7 2.8 %collective-permute-start.10 = (f16[56,2160]{1,0:T(8,128)(2,1)S(1)}, f16[56,2160]{1,0:T(8,128)(2,1)S(1)}, u32[]{:S(2)}, u32[]{:S(2)}) collective-permute-start(f16[56,2160]{1,0:T(8,128)(2,1)S(1)} %get-tuple-element.49), channel_id=1, source_target_pairs={{0,192},{1,193},{2,194},{3,195},{4,196},{5,197},{6,198},{7,199},{8... | collective-permute-start | bytes 725768 | tf_op jit(solution)/shard_map/ppermute | solution.py:30
  39.5 1.6 %collective-permute-done.17.refs_6_ = bf16[432,512]{1,0:T(8,128)(2,1)S(1)} collective-permute-done((bf16[432,512]{1,0:T(8,128)(2,1)S(1)}, bf16[432,512]{1,0:T(8,128)(2,1)S(1)}, u32[]{:S(2)}, u32[]{:S(2)}) %collective-permute-start.17) | collective-permute-done | bytes 442400 | tf_op jit(solution)/shard_map/ppermute | solution.py:30
  41.1 0.8 collective-permute-start.18
  41.9 1.2 %collective-permute-done.15.refs_4_ = bf16[432,512]{1,0:T(8,128)(2,1)S(1)} collective-permute-done((bf16[432,512]{1,0:T(8,128)(2,1)S(1)}, bf16[432,512]{1,0:T(8,128)(2,1)S(1)}, u32[]{:S(2)}, u32[]{:S(2)}) %collective-permute-start.15) | collective-permute-done | bytes 442400 | tf_op jit(solution)/shard_map/ppermute | solution.py:30
  44.4 3.1 %collective-permute-done.9 = f16[56,2160]{1,0:T(8,128)(2,1)S(1)} collective-permute-done((f16[56,2160]{1,0:T(8,128)(2,1)S(1)}, f16[56,2160]{1,0:T(8,128)(2,1)S(1)}, u32[]{:S(2)}, u32[]{:S(2)}) %collective-permute-start.9) | collective-permute-done | bytes 241952 | tf_op jit(solution)/shard_map/ppermute | solution.py:30
  48.5 2.7 %collective-permute-start.12 = (f16[2,56,2160]{2,1,0:T(8,128)(2,1)S(1)}, f16[2,56,2160]{2,1,0:T(8,128)(2,1)S(1)}, u32[]{:S(2)}, u32[]{:S(2)}) collective-permute-start(f16[2,56,2160]{2,1,0:T(8,128)(2,1)S(1)} %get-tuple-element.67), channel_id=1, source_target_pairs={{0,192},{1,193},{2,194},{3,195},{4,196},{5,197},{6,198},{7,199},{8... | collective-permute-start | bytes 1451528 | tf_op jit(solution)/shard_map/ppermute | solution.py:30
  51.2 2.7 %shard_map.29 = f32[4,2,56,1296]{3,2,1,0:T(8,128)S(1)} custom-call(bf16[432,512]{1,0:T(8,128)(2,1)S(1)} %bitcast.114, bf16[432,512]{1,0:T(8,128)(2,1)S(1)} %collective-permute-done.refs_1_, bf16[432,512]{1,0:T(8,128)(2,1)S(1)} %collective-permute-done.3.refs_4_.refs_2_, bf16[432,512]{1,0:T(8,128)(2,1)S(1)} %collective-permute-done.4.refs_5_.refs_3_, ...), custom_call_target="tpu_custom_call" | custom-call | flops 1146617856 | bytes 8388608 | tf_op jit(solution)/shard_map/pallas_call | solution.py:97
  54.2 2.7 %collective-permute-start.20 = (f16[56,1296]{1,0:T(8,128)(2,1)S(1)}, f16[56,1296]{1,0:T(8,128)(2,1)S(1)}, u32[]{:S(2)}, u32[]{:S(2)}) collective-permute-start(f16[56,1296]{1,0:T(8,128)(2,1)S(1)} %get-tuple-element.55), channel_id=1, source_target_pairs={{255,191},{254,190},{253,189},{252,188},{251,187},{250,186},{249,1... | collective-permute-start | bytes 435464 | tf_op jit(solution)/shard_map/ppermute | solution.py:30
  56.9 7.3 %collective-permute-done.19 = f16[56,1296]{1,0:T(8,128)(2,1)S(1)} collective-permute-done((f16[56,1296]{1,0:T(8,128)(2,1)S(1)}, f16[56,1296]{1,0:T(8,128)(2,1)S(1)}, u32[]{:S(2)}, u32[]{:S(2)}) %collective-permute-start.19) | collective-permute-done | bytes 145184 | tf_op jit(solution)/shard_map/ppermute | solution.py:30
  65.2 2.7 %collective-permute-start.22 = (f16[2,56,1296]{2,1,0:T(8,128)(2,1)S(1)}, f16[2,56,1296]{2,1,0:T(8,128)(2,1)S(1)}, u32[]{:S(2)}, u32[]{:S(2)}) collective-permute-start(f16[2,56,1296]{2,1,0:T(8,128)(2,1)S(1)} %get-tuple-element.65), channel_id=1, source_target_pairs={{255,191},{254,190},{253,189},{252,188},{251,187},{250,186},{249,1... | collective-permute-start | bytes 870920 | tf_op jit(solution)/shard_map/ppermute | solution.py:30
  68.9 2.8 %collective-permute-start.13 = (f16[56,2160]{1,0:T(8,128)(2,1)S(1)}, f16[56,2160]{1,0:T(8,128)(2,1)S(1)}, u32[]{:S(2)}, u32[]{:S(2)}) collective-permute-start(f16[56,2160]{1,0:T(8,128)(2,1)S(1)} %fusion.10), channel_id=1, source_target_pairs={{0,32},{1,33},{2,34},{3,35},{4,36},{5,37},{6,38},{7,39},{8,40},{9,... | collective-permute-start | bytes 725768 | tf_op jit(solution)/shard_map/ppermute | solution.py:30
  71.7 1.2 %collective-permute-done.21 = f16[2,56,1296]{2,1,0:T(8,128)(2,1)S(1)} collective-permute-done((f16[2,56,1296]{2,1,0:T(8,128)(2,1)S(1)}, f16[2,56,1296]{2,1,0:T(8,128)(2,1)S(1)}, u32[]{:S(2)}, u32[]{:S(2)}) %collective-permute-start.21) | collective-permute-done | bytes 290336 | tf_op jit(solution)/shard_map/ppermute | solution.py:30
  74.0 1.8 %collective-permute-start.25 = (f16[56,864]{1,0:T(8,128)(2,1)S(1)}, f16[56,864]{1,0:T(8,128)(2,1)S(1)}, u32[]{:S(2)}, u32[]{:S(2)}) collective-permute-start(f16[56,864]{1,0:T(8,128)(2,1)S(1)} %slice.255), channel_id=1, source_target_pairs={{0,12},{1,13},{2,14},{3,15},{4,0},{5,1},{6,2},{7,3},{8,4},{9,5},{1... | collective-permute-start | bytes 290312 | tf_op jit(solution)/shard_map/ppermute | solution.py:30
  75.8 2.7 %collective-permute-start.26 = (f16[56,864]{1,0:T(8,128)(2,1)S(1)}, f16[56,864]{1,0:T(8,128)(2,1)S(1)}, u32[]{:S(2)}, u32[]{:S(2)}) collective-permute-start(f16[56,864]{1,0:T(8,128)(2,1)S(1)} %slice.256), channel_id=1, source_target_pairs={{0,44},{1,45},{2,46},{3,47},{4,32},{5,33},{6,34},{7,35},{8,36},{9,... | collective-permute-start | bytes 290312 | tf_op jit(solution)/shard_map/ppermute | solution.py:30
  79.7 3.7 %collective-permute-start.23 = (f16[56,1296]{1,0:T(8,128)(2,1)S(1)}, f16[56,1296]{1,0:T(8,128)(2,1)S(1)}, u32[]{:S(2)}, u32[]{:S(2)}) collective-permute-start(f16[56,1296]{1,0:T(8,128)(2,1)S(1)} %pad_maximum_fusion.4), channel_id=1, source_target_pairs={{0,14},{1,15},{2,0},{3,1},{4,2},{5,3},{6,4},{7,5},{8,6},{9,7},{10,... | collective-permute-start | bytes 435464 | tf_op jit(solution)/shard_map/ppermute | solution.py:30
  83.5 1.1 %collective-permute-start.14 = (f32[56,432]{1,0:T(8,128)S(1)}, f32[56,432]{1,0:T(8,128)S(1)}, u32[]{:S(2)}, u32[]{:S(2)}) collective-permute-start(f32[56,432]{1,0:T(8,128)S(1)} %get-tuple-element.61), channel_id=1, source_target_pairs={{0,1},{1,0},{2,3},{3,2},{4,5},{5,4},{6,7},{7,6},{8,9},{9,8},{10,11... | collective-permute-start | bytes 290312 | tf_op jit(solution)/shard_map/ppermute | solution.py:30
  84.6 3.8 %collective-permute-done.23 = f16[56,1296]{1,0:T(8,128)(2,1)S(1)} collective-permute-done((f16[56,1296]{1,0:T(8,128)(2,1)S(1)}, f16[56,1296]{1,0:T(8,128)(2,1)S(1)}, u32[]{:S(2)}, u32[]{:S(2)}) %collective-permute-start.23) | collective-permute-done | bytes 145184 | tf_op jit(solution)/shard_map/ppermute | solution.py:30
  90.1 3.0 %collective-permute-start.27 = (f32[27,3456]{1,0:T(8,128)S(1)}, f32[27,3456]{1,0:T(8,128)S(1)}, u32[]{:S(2)}, u32[]{:S(2)}) collective-permute-start(f32[27,3456]{1,0:T(8,128)S(1)} %constant_dynamic-slice_fusion.3), channel_id=1, source_target_pairs={{0,16},{1,17},{2,18},{3,19},{4,20},{5,21},{6,22},{7,23},{8,24},{9,... | collective-permute-start | bytes 1119752 | tf_op jit(solution)/shard_map/ppermute | solution.py:30
  93.1 1.4 %collective-permute-done.27.theirs = f32[27,3456]{1,0:T(8,128)S(1)} collective-permute-done((f32[27,3456]{1,0:T(8,128)S(1)}, f32[27,3456]{1,0:T(8,128)S(1)}, u32[]{:S(2)}, u32[]{:S(2)}) %collective-permute-start.27) | collective-permute-done | bytes 373280 | tf_op jit(solution)/shard_map/ppermute | solution.py:30
  94.5 1.6 %shard_map.30 = f32[27,6912]{1,0:T(8,128)} custom-call(f32[56,3456]{1,0:T(8,128)S(1)} %concatenate.7.mine, f32[27,3456]{1,0:T(8,128)S(1)} %collective-permute-done.27.theirs, f32[27,6912]{1,0:T(8,128)S(1)} %copy-done.1), custom_call_target="tpu_custom_call" | custom-call | bytes 4194304 | tf_op jit(solution)/shard_map/pallas_call | solution.py:202
  (100 shorter events, 9.1 us)
Async XLA Ops:
  0.0 15.6 %collective-permute-start.1 = (bf16[432,512]{1,0:T(8,128)(2,1)}, bf16[432,512]{1,0:T(8,128)(2,1)S(1)}, u32[]{:S(2)}, u32[]{:S(2)}) collective-permute-start(bf16[432,512]{1,0:T(8,128)(2,1)} %bitcast.109), channel_id=1, source_target_pairs={{0,14},{1,15},{2,0},{3,1},{4,2},{5,3},{6,4},{7,5},{8,6},{9,7},{10,... | collective-permute-start | bytes 1327112 | tf_op jit(solution)/shard_map/ppermute | solution.py:30
  6.4 12.5 %collective-permute-start = (bf16[432,512]{1,0:T(8,128)(2,1)}, bf16[432,512]{1,0:T(8,128)(2,1)S(1)}, u32[]{:S(2)}, u32[]{:S(2)}) collective-permute-start(bf16[432,512]{1,0:T(8,128)(2,1)} %bitcast.110), channel_id=1, source_target_pairs={{0,16},{1,17},{2,18},{3,19},{4,20},{5,21},{6,22},{7,23},{8,24},{9,... | collective-permute-start | bytes 1327112 | tf_op jit(solution)/shard_map/ppermute | solution.py:30
  7.4 13.2 %collective-permute-start.3 = (bf16[432,512]{1,0:T(8,128)(2,1)}, bf16[432,512]{1,0:T(8,128)(2,1)S(1)}, u32[]{:S(2)}, u32[]{:S(2)}) collective-permute-start(bf16[432,512]{1,0:T(8,128)(2,1)} %bitcast.111), channel_id=1, source_target_pairs={{0,2},{1,3},{2,4},{3,5},{4,6},{5,7},{6,8},{7,9},{8,10},{9,11},{10,... | collective-permute-start | bytes 1327112 | tf_op jit(solution)/shard_map/ppermute | solution.py:30
  7.4 14.0 %collective-permute-start.5 = (bf16[432,512]{1,0:T(8,128)(2,1)}, bf16[432,512]{1,0:T(8,128)(2,1)S(1)}, u32[]{:S(2)}, u32[]{:S(2)}) collective-permute-start(bf16[432,512]{1,0:T(8,128)(2,1)} %bitcast.112), channel_id=1, source_target_pairs={{0,1},{1,0},{2,3},{3,2},{4,5},{5,4},{6,7},{7,6},{8,9},{9,8},{10,11... | collective-permute-start | bytes 1327112 | tf_op jit(solution)/shard_map/ppermute | solution.py:30
  15.6 11.2 %collective-permute-start.7 = (bf16[432,512]{1,0:T(8,128)(2,1)S(1)}, bf16[432,512]{1,0:T(8,128)(2,1)S(1)}, u32[]{:S(2)}, u32[]{:S(2)}) collective-permute-start(bf16[432,512]{1,0:T(8,128)(2,1)S(1)} %collective-permute-done.1.refs_2_), channel_id=1, source_target_pairs={{0,14},{1,15},{2,0},{3,1},{4,2},{5,3},{6,4},{7,5},{8,6},{9,7},{10,... | collective-permute-start | bytes 1327112 | tf_op jit(solution)/shard_map/ppermute | solution.py:30
  20.6 8.7 %collective-permute-start.4 = (bf16[432,512]{1,0:T(8,128)(2,1)S(1)}, bf16[432,512]{1,0:T(8,128)(2,1)S(1)}, u32[]{:S(2)}, u32[]{:S(2)}) collective-permute-start(bf16[432,512]{1,0:T(8,128)(2,1)S(1)} %collective-permute-done.3.refs_4_.refs_2_), channel_id=1, source_target_pairs={{0,16},{1,17},{2,18},{3,19},{4,20},{5,21},{6,22},{7,23},{8,24},{9,... | collective-permute-start | bytes 1327112 | tf_op jit(solution)/shard_map/ppermute | solution.py:30
  21.4 9.2 %collective-permute-start.2 = (bf16[432,512]{1,0:T(8,128)(2,1)S(1)}, bf16[432,512]{1,0:T(8,128)(2,1)S(1)}, u32[]{:S(2)}, u32[]{:S(2)}) collective-permute-start(bf16[432,512]{1,0:T(8,128)(2,1)S(1)} %collective-permute-done.1.refs_2_), channel_id=1, source_target_pairs={{0,16},{1,17},{2,18},{3,19},{4,20},{5,21},{6,22},{7,23},{8,24},{9,... | collective-permute-start | bytes 1327112 | tf_op jit(solution)/shard_map/ppermute | solution.py:30
  21.4 9.2 %collective-permute-start.6 = (bf16[432,512]{1,0:T(8,128)(2,1)S(1)}, bf16[432,512]{1,0:T(8,128)(2,1)}, u32[]{:S(2)}, u32[]{:S(2)}) collective-permute-start(bf16[432,512]{1,0:T(8,128)(2,1)S(1)} %collective-permute-done.5.refs_6_), channel_id=1, source_target_pairs={{0,16},{1,17},{2,18},{3,19},{4,20},{5,21},{6,22},{7,23},{8,24},{9,... | collective-permute-start | bytes 1327112 | tf_op jit(solution)/shard_map/ppermute | solution.py:30
  26.8 3.9 %collective-permute-start.8 = (bf16[432,512]{1,0:T(8,128)(2,1)S(1)}, bf16[432,512]{1,0:T(8,128)(2,1)S(1)}, u32[]{:S(2)}, u32[]{:S(2)}) collective-permute-start(bf16[432,512]{1,0:T(8,128)(2,1)S(1)} %collective-permute-done.7.refs_8_), channel_id=1, source_target_pairs={{0,16},{1,17},{2,18},{3,19},{4,20},{5,21},{6,22},{7,23},{8,24},{9,... | collective-permute-start | bytes 1327112 | tf_op jit(solution)/shard_map/ppermute | solution.py:30
  29.3 13.9 %collective-permute-start.15 = (bf16[432,512]{1,0:T(8,128)(2,1)S(1)}, bf16[432,512]{1,0:T(8,128)(2,1)S(1)}, u32[]{:S(2)}, u32[]{:S(2)}) collective-permute-start(bf16[432,512]{1,0:T(8,128)(2,1)S(1)} %collective-permute-done.3.refs_4_.refs_2_), channel_id=1, source_target_pairs={{0,2},{1,3},{2,4},{3,5},{4,6},{5,7},{6,8},{7,9},{8,10},{9,11},{10,... | collective-permute-start | bytes 1327112 | tf_op jit(solution)/shard_map/ppermute | solution.py:30
  29.3 11.9 %collective-permute-start.17 = (bf16[432,512]{1,0:T(8,128)(2,1)S(1)}, bf16[432,512]{1,0:T(8,128)(2,1)S(1)}, u32[]{:S(2)}, u32[]{:S(2)}) collective-permute-start(bf16[432,512]{1,0:T(8,128)(2,1)S(1)} %collective-permute-done.7.refs_8_), channel_id=1, source_target_pairs={{0,1},{1,0},{2,3},{3,2},{4,5},{5,4},{6,7},{7,6},{8,9},{9,8},{10,11... | collective-permute-start | bytes 1327112 | tf_op jit(solution)/shard_map/ppermute | solution.py:30
  30.7 1.0 %copy-start = (bf16[512,432]{0,1:T(8,128)(2,1)S(1)}, bf16[512,432]{0,1:T(8,128)(2,1)}, u32[]{:S(2)}) copy-start(bf16[512,432]{0,1:T(8,128)(2,1)} %param.2) | copy-start | bytes 1327108
  36.7 7.7 %collective-permute-start.10 = (f16[56,2160]{1,0:T(8,128)(2,1)S(1)}, f16[56,2160]{1,0:T(8,128)(2,1)S(1)}, u32[]{:S(2)}, u32[]{:S(2)}) collective-permute-start(f16[56,2160]{1,0:T(8,128)(2,1)S(1)} %get-tuple-element.49), channel_id=1, source_target_pairs={{0,192},{1,193},{2,194},{3,195},{4,196},{5,197},{6,198},{7,199},{8... | collective-permute-start | bytes 725768 | tf_op jit(solution)/shard_map/ppermute | solution.py:30
  39.5 8.0 %collective-permute-start.9 = (f16[56,2160]{1,0:T(8,128)(2,1)S(1)}, f16[56,2160]{1,0:T(8,128)(2,1)S(1)}, u32[]{:S(2)}, u32[]{:S(2)}) collective-permute-start(f16[56,2160]{1,0:T(8,128)(2,1)S(1)} %get-tuple-element.50), channel_id=1, source_target_pairs={{0,64},{1,65},{2,66},{3,67},{4,68},{5,69},{6,70},{7,71},{8,72},{9,... | collective-permute-start | bytes 725768 | tf_op jit(solution)/shard_map/ppermute | solution.py:30
  41.1 10.1 %collective-permute-start.18 = (bf16[432,512]{1,0:T(8,128)(2,1)S(1)}, bf16[432,512]{1,0:T(8,128)(2,1)S(1)}, u32[]{:S(2)}, u32[]{:S(2)}) collective-permute-start(bf16[432,512]{1,0:T(8,128)(2,1)S(1)} %collective-permute-done.17.refs_6_), channel_id=1, source_target_pairs={{0,16},{1,17},{2,18},{3,19},{4,20},{5,21},{6,22},{7,23},{8,24},{9,... | collective-permute-start | bytes 1327112 | tf_op jit(solution)/shard_map/ppermute | solution.py:30
  43.1 8.1 %collective-permute-start.16 = (bf16[432,512]{1,0:T(8,128)(2,1)S(1)}, bf16[432,512]{1,0:T(8,128)(2,1)S(1)}, u32[]{:S(2)}, u32[]{:S(2)}) collective-permute-start(bf16[432,512]{1,0:T(8,128)(2,1)S(1)} %collective-permute-done.15.refs_4_), channel_id=1, source_target_pairs={{0,16},{1,17},{2,18},{3,19},{4,20},{5,21},{6,22},{7,23},{8,24},{9,... | collective-permute-start | bytes 1327112 | tf_op jit(solution)/shard_map/ppermute | solution.py:30
  48.4 19.5 %collective-permute-start.11 = (f16[2,56,2160]{2,1,0:T(8,128)(2,1)S(1)}, f16[2,56,2160]{2,1,0:T(8,128)(2,1)S(1)}, u32[]{:S(2)}, u32[]{:S(2)}) collective-permute-start(f16[2,56,2160]{2,1,0:T(8,128)(2,1)S(1)} %get-tuple-element.68), channel_id=1, source_target_pairs={{0,64},{1,65},{2,66},{3,67},{4,68},{5,69},{6,70},{7,71},{8,72},{9,... | collective-permute-start | bytes 1451528 | tf_op jit(solution)/shard_map/ppermute | solution.py:30
  48.5 19.4 %collective-permute-start.12 = (f16[2,56,2160]{2,1,0:T(8,128)(2,1)S(1)}, f16[2,56,2160]{2,1,0:T(8,128)(2,1)S(1)}, u32[]{:S(2)}, u32[]{:S(2)}) collective-permute-start(f16[2,56,2160]{2,1,0:T(8,128)(2,1)S(1)} %get-tuple-element.67), channel_id=1, source_target_pairs={{0,192},{1,193},{2,194},{3,195},{4,196},{5,197},{6,198},{7,199},{8... | collective-permute-start | bytes 1451528 | tf_op jit(solution)/shard_map/ppermute | solution.py:30
  54.1 10.1 %collective-permute-start.19 = (f16[56,1296]{1,0:T(8,128)(2,1)S(1)}, f16[56,1296]{1,0:T(8,128)(2,1)S(1)}, u32[]{:S(2)}, u32[]{:S(2)}) collective-permute-start(f16[56,1296]{1,0:T(8,128)(2,1)S(1)} %get-tuple-element.56), channel_id=1, source_target_pairs={{255,63},{254,62},{253,61},{252,60},{251,59},{250,58},{249,57},{24... | collective-permute-start | bytes 435464 | tf_op jit(solution)/shard_map/ppermute | solution.py:30
  54.2 10.0 %collective-permute-start.20 = (f16[56,1296]{1,0:T(8,128)(2,1)S(1)}, f16[56,1296]{1,0:T(8,128)(2,1)S(1)}, u32[]{:S(2)}, u32[]{:S(2)}) collective-permute-start(f16[56,1296]{1,0:T(8,128)(2,1)S(1)} %get-tuple-element.55), channel_id=1, source_target_pairs={{255,191},{254,190},{253,189},{252,188},{251,187},{250,186},{249,1... | collective-permute-start | bytes 435464 | tf_op jit(solution)/shard_map/ppermute | solution.py:30
  64.9 8.0 %collective-permute-start.21 = (f16[2,56,1296]{2,1,0:T(8,128)(2,1)S(1)}, f16[2,56,1296]{2,1,0:T(8,128)(2,1)S(1)}, u32[]{:S(2)}, u32[]{:S(2)}) collective-permute-start(f16[2,56,1296]{2,1,0:T(8,128)(2,1)S(1)} %get-tuple-element.66), channel_id=1, source_target_pairs={{255,63},{254,62},{253,61},{252,60},{251,59},{250,58},{249,57},{24... | collective-permute-start | bytes 870920 | tf_op jit(solution)/shard_map/ppermute | solution.py:30
  65.2 7.7 %collective-permute-start.22 = (f16[2,56,1296]{2,1,0:T(8,128)(2,1)S(1)}, f16[2,56,1296]{2,1,0:T(8,128)(2,1)S(1)}, u32[]{:S(2)}, u32[]{:S(2)}) collective-permute-start(f16[2,56,1296]{2,1,0:T(8,128)(2,1)S(1)} %get-tuple-element.65), channel_id=1, source_target_pairs={{255,191},{254,190},{253,189},{252,188},{251,187},{250,186},{249,1... | collective-permute-start | bytes 870920 | tf_op jit(solution)/shard_map/ppermute | solution.py:30
  68.9 10.2 %collective-permute-start.13 = (f16[56,2160]{1,0:T(8,128)(2,1)S(1)}, f16[56,2160]{1,0:T(8,128)(2,1)S(1)}, u32[]{:S(2)}, u32[]{:S(2)}) collective-permute-start(f16[56,2160]{1,0:T(8,128)(2,1)S(1)} %fusion.10), channel_id=1, source_target_pairs={{0,32},{1,33},{2,34},{3,35},{4,36},{5,37},{6,38},{7,39},{8,40},{9,... | collective-permute-start | bytes 725768 | tf_op jit(solution)/shard_map/ppermute | solution.py:30
  74.0 10.6 %collective-permute-start.25 = (f16[56,864]{1,0:T(8,128)(2,1)S(1)}, f16[56,864]{1,0:T(8,128)(2,1)S(1)}, u32[]{:S(2)}, u32[]{:S(2)}) collective-permute-start(f16[56,864]{1,0:T(8,128)(2,1)S(1)} %slice.255), channel_id=1, source_target_pairs={{0,12},{1,13},{2,14},{3,15},{4,0},{5,1},{6,2},{7,3},{8,4},{9,5},{1... | collective-permute-start | bytes 290312 | tf_op jit(solution)/shard_map/ppermute | solution.py:30
  75.8 8.8 %collective-permute-start.26 = (f16[56,864]{1,0:T(8,128)(2,1)S(1)}, f16[56,864]{1,0:T(8,128)(2,1)S(1)}, u32[]{:S(2)}, u32[]{:S(2)}) collective-permute-start(f16[56,864]{1,0:T(8,128)(2,1)S(1)} %slice.256), channel_id=1, source_target_pairs={{0,44},{1,45},{2,46},{3,47},{4,32},{5,33},{6,34},{7,35},{8,36},{9,... | collective-permute-start | bytes 290312 | tf_op jit(solution)/shard_map/ppermute | solution.py:30
  78.5 6.1 %collective-permute-start.24 = (f16[56,432]{1,0:T(8,128)(2,1)S(1)}, f16[56,432]{1,0:T(8,128)(2,1)S(1)}, u32[]{:S(2)}, u32[]{:S(2)}) collective-permute-start(f16[56,432]{1,0:T(8,128)(2,1)S(1)} %slice.254), channel_id=1, source_target_pairs={{0,46},{1,47},{2,32},{3,33},{4,34},{5,35},{6,36},{7,37},{8,38},{9,... | collective-permute-start | bytes 145160 | tf_op jit(solution)/shard_map/ppermute | solution.py:30
  79.1 15.4 %copy-start.1 = (f32[27,6912]{1,0:T(8,128)S(1)}, f32[27,6912]{1,0:T(8,128)}, u32[]{:S(2)}) copy-start(f32[27,6912]{1,0:T(8,128)} %previous.1) | copy-start | bytes 2239492
  79.7 8.8 %collective-permute-start.23 = (f16[56,1296]{1,0:T(8,128)(2,1)S(1)}, f16[56,1296]{1,0:T(8,128)(2,1)S(1)}, u32[]{:S(2)}, u32[]{:S(2)}) collective-permute-start(f16[56,1296]{1,0:T(8,128)(2,1)S(1)} %pad_maximum_fusion.4), channel_id=1, source_target_pairs={{0,14},{1,15},{2,0},{3,1},{4,2},{5,3},{6,4},{7,5},{8,6},{9,7},{10,... | collective-permute-start | bytes 435464 | tf_op jit(solution)/shard_map/ppermute | solution.py:30
  83.5 6.2 %collective-permute-start.14 = (f32[56,432]{1,0:T(8,128)S(1)}, f32[56,432]{1,0:T(8,128)S(1)}, u32[]{:S(2)}, u32[]{:S(2)}) collective-permute-start(f32[56,432]{1,0:T(8,128)S(1)} %get-tuple-element.61), channel_id=1, source_target_pairs={{0,1},{1,0},{2,3},{3,2},{4,5},{5,4},{6,7},{7,6},{8,9},{9,8},{10,11... | collective-permute-start | bytes 290312 | tf_op jit(solution)/shard_map/ppermute | solution.py:30
  90.1 4.4 %collective-permute-start.27 = (f32[27,3456]{1,0:T(8,128)S(1)}, f32[27,3456]{1,0:T(8,128)S(1)}, u32[]{:S(2)}, u32[]{:S(2)}) collective-permute-start(f32[27,3456]{1,0:T(8,128)S(1)} %constant_dynamic-slice_fusion.3), channel_id=1, source_target_pairs={{0,16},{1,17},{2,18},{3,19},{4,20},{5,21},{6,22},{7,23},{8,24},{9,... | collective-permute-start | bytes 1119752 | tf_op jit(solution)/shard_map/ppermute | solution.py:30

commit v2 on v1

--- a/solution.py
+++ b/solution.py
@@ -232,7 +232,8 @@
     )
     far1 = y_first(part1, rows, y_at)
     half1 = along_y(far1[0], 1), along_y(far1[1], -1)
-    across2_2, before2_2 = other_core(tied(across2, *far1)), other_core(tied(before2, *far1))
+    across2_2 = other_core(tied(across2, *far1))
+    before2_2 = other_core(tied(before2, *half1))
 
     far = [(own, own_2), (before, before_2), (before2, before2_2), (across2, across2_2), (after2, after2_2)]
     part2 = products((((1, 3), (2, 4), (2, 3)), ((0, 3), (3, 0), (3, 1))), far)

time: 96.2 us -> 100 us (1.040)
  waiting for transfers between devices: 34.6 us -> 38.9 us
    ppermute x28, waiting for transfers between devices: 34.6 us -> 38.9 us  [move(): return lax.ppermute(value, AXES, pairs[::-1] if turned else pairs)]
  transfers between devices with their start and end apart: 28 -> 28, of which waited for: 13 -> 12; matrix products, arithmetic and copies ran while one was open for 5% -> 4% of each run, Pallas kernels for 8% -> 7%
where the time goes in v2:
time: 100 us
  starting transfers between devices  45.1 us (45%)
  waiting for transfers between devices  38.9 us (39%)
  Pallas kernels  8.95 us (9%)
  other arithmetic  4.65 us (5%)
  local copies, waits for them, and re-layouts  1.98 us (2%)
    ppermute x28, starting transfers between devices, move(): return lax.ppermute(value, AXES, pairs[::-1] if turned else pairs)  45.1 us
    ppermute x28, waiting for transfers between devices, move(): return lax.ppermute(value, AXES, pairs[::-1] if turned else pairs)  38.9 us
    pallas_call x2, Pallas kernels, products(): pl.pallas_call(functools.partial(products_kernel, units, len(shards), wid...  7.4 us
  transfers between devices with their start and end apart: 28, of which 12 were waited for; matrix products, arithmetic and copies ran while one was open for 4% of the time, Pallas kernels for 7%

profile of v2, /device:TPU:1, one launch (start us, length us, event | category | flops | bytes accessed | tf_op | source)
XLA Modules:
  0.0 100.1 jit_solution(7677566157703084016)
XLA Ops:
  0.0 6.4 %collective-permute-start.1 = (bf16[432,512]{1,0:T(8,128)(2,1)}, bf16[432,512]{1,0:T(8,128)(2,1)S(1)}, u32[]{:S(2)}, u32[]{:S(2)}) collective-permute-start(bf16[432,512]{1,0:T(8,128)(2,1)} %bitcast.109), channel_id=1, source_target_pairs={{0,14},{1,15},{2,0},{3,1},{4,2},{5,3},{6,4},{7,5},{8,6},{9,7},{10,... | collective-permute-start | bytes 1327112 | tf_op jit(solution)/shard_map/ppermute | solution.py:30
  6.4 1.0 collective-permute-start
  7.4 1.2 %collective-permute-start.5 = (bf16[432,512]{1,0:T(8,128)(2,1)}, bf16[432,512]{1,0:T(8,128)(2,1)S(1)}, u32[]{:S(2)}, u32[]{:S(2)}) collective-permute-start(bf16[432,512]{1,0:T(8,128)(2,1)} %bitcast.112), channel_id=1, source_target_pairs={{0,1},{1,0},{2,3},{3,2},{4,5},{5,4},{6,7},{7,6},{8,9},{9,8},{10,11... | collective-permute-start | bytes 1327112 | tf_op jit(solution)/shard_map/ppermute | solution.py:30
  8.6 7.0 %collective-permute-done.1.refs_2_ = bf16[432,512]{1,0:T(8,128)(2,1)S(1)} collective-permute-done((bf16[432,512]{1,0:T(8,128)(2,1)}, bf16[432,512]{1,0:T(8,128)(2,1)S(1)}, u32[]{:S(2)}, u32[]{:S(2)}) %collective-permute-start.1) | collective-permute-done | bytes 442400 | tf_op jit(solution)/shard_map/ppermute | solution.py:30
  15.6 3.3 %collective-permute-start.7 = (bf16[432,512]{1,0:T(8,128)(2,1)S(1)}, bf16[432,512]{1,0:T(8,128)(2,1)S(1)}, u32[]{:S(2)}, u32[]{:S(2)}) collective-permute-start(bf16[432,512]{1,0:T(8,128)(2,1)S(1)} %collective-permute-done.1.refs_2_), channel_id=1, source_target_pairs={{0,14},{1,15},{2,0},{3,1},{4,2},{5,3},{6,4},{7,5},{8,6},{9,7},{10,... | collective-permute-start | bytes 1327112 | tf_op jit(solution)/shard_map/ppermute | solution.py:30
  18.9 1.7 %collective-permute-done.3.refs_4_.refs_2_ = bf16[432,512]{1,0:T(8,128)(2,1)S(1)} collective-permute-done((bf16[432,512]{1,0:T(8,128)(2,1)}, bf16[432,512]{1,0:T(8,128)(2,1)S(1)}, u32[]{:S(2)}, u32[]{:S(2)}) %collective-permute-start.3) | collective-permute-done | bytes 442400 | tf_op jit(solution)/shard_map/ppermute | solution.py:30
  21.9 4.9 %collective-permute-done.7.refs_8_ = bf16[432,512]{1,0:T(8,128)(2,1)S(1)} collective-permute-done((bf16[432,512]{1,0:T(8,128)(2,1)S(1)}, bf16[432,512]{1,0:T(8,128)(2,1)S(1)}, u32[]{:S(2)}, u32[]{:S(2)}) %collective-permute-start.7) | collective-permute-done | bytes 442400 | tf_op jit(solution)/shard_map/ppermute | solution.py:30
  26.8 2.5 %collective-permute-start.8 = (bf16[432,512]{1,0:T(8,128)(2,1)S(1)}, bf16[432,512]{1,0:T(8,128)(2,1)S(1)}, u32[]{:S(2)}, u32[]{:S(2)}) collective-permute-start(bf16[432,512]{1,0:T(8,128)(2,1)S(1)} %collective-permute-done.7.refs_8_), channel_id=1, source_target_pairs={{0,16},{1,17},{2,18},{3,19},{4,20},{5,21},{6,22},{7,23},{8,24},{9,... | collective-permute-start | bytes 1327112 | tf_op jit(solution)/shard_map/ppermute | solution.py:30
  29.3 1.3 %collective-permute-start.17 = (bf16[432,512]{1,0:T(8,128)(2,1)S(1)}, bf16[432,512]{1,0:T(8,128)(2,1)S(1)}, u32[]{:S(2)}, u32[]{:S(2)}) collective-permute-start(bf16[432,512]{1,0:T(8,128)(2,1)S(1)} %collective-permute-done.7.refs_8_), channel_id=1, source_target_pairs={{0,1},{1,0},{2,3},{3,2},{4,5},{5,4},{6,7},{7,6},{8,9},{9,8},{10,11... | collective-permute-start | bytes 1327112 | tf_op jit(solution)/shard_map/ppermute | solution.py:30
  30.7 1.0 %copy-done = bf16[512,432]{0,1:T(8,128)(2,1)S(1)} copy-done((bf16[512,432]{0,1:T(8,128)(2,1)S(1)}, bf16[512,432]{0,1:T(8,128)(2,1)}, u32[]{:S(2)}) %copy-start) | copy-done | bytes 442392
  31.7 4.7 %shard_map.28 = f32[4,2,56,2160]{3,2,1,0:T(8,128)S(1)} custom-call(bf16[432,512]{1,0:T(8,128)(2,1)S(1)} %bitcast.113, bf16[432,512]{1,0:T(8,128)(2,1)S(1)} %collective-permute-done.refs_1_, bf16[432,512]{1,0:T(8,128)(2,1)S(1)} %collective-permute-done.1.refs_2_, bf16[432,512]{1,0:T(8,128)(2,1)S(1)} %collective-permute-done.2.refs_3_, ...), custom_call_target="tpu_custom_call" | custom-call | flops 1911029760 | bytes 8388608 | tf_op jit(solution)/shard_map/pallas_call | solution.py:97
  36.7 2.8 %collective-permute-start.10 = (f16[56,2160]{1,0:T(8,128)(2,1)S(1)}, f16[56,2160]{1,0:T(8,128)(2,1)S(1)}, u32[]{:S(2)}, u32[]{:S(2)}) collective-permute-start(f16[56,2160]{1,0:T(8,128)(2,1)S(1)} %get-tuple-element.49), channel_id=1, source_target_pairs={{0,192},{1,193},{2,194},{3,195},{4,196},{5,197},{6,198},{7,199},{8... | collective-permute-start | bytes 725768 | tf_op jit(solution)/shard_map/ppermute | solution.py:30
  39.5 1.6 %collective-permute-done.17.refs_6_ = bf16[432,512]{1,0:T(8,128)(2,1)S(1)} collective-permute-done((bf16[432,512]{1,0:T(8,128)(2,1)S(1)}, bf16[432,512]{1,0:T(8,128)(2,1)S(1)}, u32[]{:S(2)}, u32[]{:S(2)}) %collective-permute-start.17) | collective-permute-done | bytes 442400 | tf_op jit(solution)/shard_map/ppermute | solution.py:30
  41.1 0.8 collective-permute-start.18
  42.0 2.4 %collective-permute-done.10 = f16[56,2160]{1,0:T(8,128)(2,1)S(1)} collective-permute-done((f16[56,2160]{1,0:T(8,128)(2,1)S(1)}, f16[56,2160]{1,0:T(8,128)(2,1)S(1)}, u32[]{:S(2)}, u32[]{:S(2)}) %collective-permute-start.10) | collective-permute-done | bytes 241952 | tf_op jit(solution)/shard_map/ppermute | solution.py:30
  44.4 3.1 %collective-permute-done.9 = f16[56,2160]{1,0:T(8,128)(2,1)S(1)} collective-permute-done((f16[56,2160]{1,0:T(8,128)(2,1)S(1)}, f16[56,2160]{1,0:T(8,128)(2,1)S(1)}, u32[]{:S(2)}, u32[]{:S(2)}) %collective-permute-start.9) | collective-permute-done | bytes 241952 | tf_op jit(solution)/shard_map/ppermute | solution.py:30
  48.1 1.6 %collective-permute-start.16 = (bf16[432,512]{1,0:T(8,128)(2,1)S(1)}, bf16[432,512]{1,0:T(8,128)(2,1)S(1)}, u32[]{:S(2)}, u32[]{:S(2)}) collective-permute-start(bf16[432,512]{1,0:T(8,128)(2,1)S(1)} %collective-permute-done.15.refs_4_), channel_id=1, source_target_pairs={{0,16},{1,17},{2,18},{3,19},{4,20},{5,21},{6,22},{7,23},{8,24},{9,... | collective-permute-start | bytes 1327112 | tf_op jit(solution)/shard_map/ppermute | solution.py:30
  50.2 2.7 %collective-permute-start.12 = (f16[2,56,2160]{2,1,0:T(8,128)(2,1)S(1)}, f16[2,56,2160]{2,1,0:T(8,128)(2,1)S(1)}, u32[]{:S(2)}, u32[]{:S(2)}) collective-permute-start(f16[2,56,2160]{2,1,0:T(8,128)(2,1)S(1)} %get-tuple-element.67), channel_id=1, source_target_pairs={{0,192},{1,193},{2,194},{3,195},{4,196},{5,197},{6,198},{7,199},{8... | collective-permute-start | bytes 1451528 | tf_op jit(solution)/shard_map/ppermute | solution.py:30
  52.8 2.7 %shard_map.29 = f32[4,2,56,1296]{3,2,1,0:T(8,128)S(1)} custom-call(bf16[432,512]{1,0:T(8,128)(2,1)S(1)} %bitcast.114, bf16[432,512]{1,0:T(8,128)(2,1)S(1)} %collective-permute-done.refs_1_, bf16[432,512]{1,0:T(8,128)(2,1)S(1)} %collective-permute-done.3.refs_4_.refs_2_, bf16[432,512]{1,0:T(8,128)(2,1)S(1)} %collective-permute-done.4.refs_5_.refs_3_, ...), custom_call_target="tpu_custom_call" | custom-call | flops 1146617856 | bytes 8388608 | tf_op jit(solution)/shard_map/pallas_call | solution.py:97
  55.8 2.7 %collective-permute-start.20 = (f16[56,1296]{1,0:T(8,128)(2,1)S(1)}, f16[56,1296]{1,0:T(8,128)(2,1)S(1)}, u32[]{:S(2)}, u32[]{:S(2)}) collective-permute-start(f16[56,1296]{1,0:T(8,128)(2,1)S(1)} %get-tuple-element.55), channel_id=1, source_target_pairs={{255,191},{254,190},{253,189},{252,188},{251,187},{250,186},{249,1... | collective-permute-start | bytes 435464 | tf_op jit(solution)/shard_map/ppermute | solution.py:30
  58.6 5.6 %collective-permute-done.11 = f16[2,56,2160]{2,1,0:T(8,128)(2,1)S(1)} collective-permute-done((f16[2,56,2160]{2,1,0:T(8,128)(2,1)S(1)}, f16[2,56,2160]{2,1,0:T(8,128)(2,1)S(1)}, u32[]{:S(2)}, u32[]{:S(2)}) %collective-permute-start.11) | collective-permute-done | bytes 483872 | tf_op jit(solution)/shard_map/ppermute | solution.py:30
  65.1 3.1 %collective-permute-start.13 = (f16[56,2160]{1,0:T(8,128)(2,1)S(1)}, f16[56,2160]{1,0:T(8,128)(2,1)S(1)}, u32[]{:S(2)}, u32[]{:S(2)}) collective-permute-start(f16[56,2160]{1,0:T(8,128)(2,1)S(1)} %fusion.10), channel_id=1, source_target_pairs={{0,32},{1,33},{2,34},{3,35},{4,36},{5,37},{6,38},{7,39},{8,40},{9,... | collective-permute-start | bytes 725768 | tf_op jit(solution)/shard_map/ppermute | solution.py:30
  68.9 2.7 %collective-permute-start.22 = (f16[2,56,1296]{2,1,0:T(8,128)(2,1)S(1)}, f16[2,56,1296]{2,1,0:T(8,128)(2,1)S(1)}, u32[]{:S(2)}, u32[]{:S(2)}) collective-permute-start(f16[2,56,1296]{2,1,0:T(8,128)(2,1)S(1)} %get-tuple-element.65), channel_id=1, source_target_pairs={{255,191},{254,190},{253,189},{252,188},{251,187},{250,186},{249,1... | collective-permute-start | bytes 870920 | tf_op jit(solution)/shard_map/ppermute | solution.py:30
  71.6 1.5 %collective-permute-done.13 = f16[56,2160]{1,0:T(8,128)(2,1)S(1)} collective-permute-done((f16[56,2160]{1,0:T(8,128)(2,1)S(1)}, f16[56,2160]{1,0:T(8,128)(2,1)S(1)}, u32[]{:S(2)}, u32[]{:S(2)}) %collective-permute-start.13) | collective-permute-done | bytes 241952 | tf_op jit(solution)/shard_map/ppermute | solution.py:30
  73.6 4.0 %collective-permute-done.21 = f16[2,56,1296]{2,1,0:T(8,128)(2,1)S(1)} collective-permute-done((f16[2,56,1296]{2,1,0:T(8,128)(2,1)S(1)}, f16[2,56,1296]{2,1,0:T(8,128)(2,1)S(1)}, u32[]{:S(2)}, u32[]{:S(2)}) %collective-permute-start.21) | collective-permute-done | bytes 290336 | tf_op jit(solution)/shard_map/ppermute | solution.py:30
  78.8 2.4 %collective-permute-start.23 = (f16[56,1296]{1,0:T(8,128)(2,1)S(1)}, f16[56,1296]{1,0:T(8,128)(2,1)S(1)}, u32[]{:S(2)}, u32[]{:S(2)}) collective-permute-start(f16[56,1296]{1,0:T(8,128)(2,1)S(1)} %pad_maximum_fusion.4), channel_id=1, source_target_pairs={{0,14},{1,15},{2,0},{3,1},{4,2},{5,3},{6,4},{7,5},{8,6},{9,7},{10,... | collective-permute-start | bytes 435464 | tf_op jit(solution)/shard_map/ppermute | solution.py:30
  81.2 0.8 collective-permute-start.25
  82.0 5.9 %collective-permute-start.26 = (f16[56,864]{1,0:T(8,128)(2,1)S(1)}, f16[56,864]{1,0:T(8,128)(2,1)S(1)}, u32[]{:S(2)}, u32[]{:S(2)}) collective-permute-start(f16[56,864]{1,0:T(8,128)(2,1)S(1)} %slice.256), channel_id=1, source_target_pairs={{0,44},{1,45},{2,46},{3,47},{4,32},{5,33},{6,34},{7,35},{8,36},{9,... | collective-permute-start | bytes 290312 | tf_op jit(solution)/shard_map/ppermute | solution.py:30
  88.7 5.6 %collective-permute-done.24 = f16[56,432]{1,0:T(8,128)(2,1)S(1)} collective-permute-done((f16[56,432]{1,0:T(8,128)(2,1)S(1)}, f16[56,432]{1,0:T(8,128)(2,1)S(1)}, u32[]{:S(2)}, u32[]{:S(2)}) %collective-permute-start.24) | collective-permute-done | bytes 48416 | tf_op jit(solution)/shard_map/ppermute | solution.py:30
  95.3 1.8 %collective-permute-start.27 = (f32[27,3456]{1,0:T(8,128)S(1)}, f32[27,3456]{1,0:T(8,128)S(1)}, u32[]{:S(2)}, u32[]{:S(2)}) collective-permute-start(f32[27,3456]{1,0:T(8,128)S(1)} %constant_dynamic-slice_fusion.3), channel_id=1, source_target_pairs={{0,16},{1,17},{2,18},{3,19},{4,20},{5,21},{6,22},{7,23},{8,24},{9,... | collective-permute-start | bytes 1119752 | tf_op jit(solution)/shard_map/ppermute | solution.py:30
  97.1 1.4 %collective-permute-done.27.theirs = f32[27,3456]{1,0:T(8,128)S(1)} collective-permute-done((f32[27,3456]{1,0:T(8,128)S(1)}, f32[27,3456]{1,0:T(8,128)S(1)}, u32[]{:S(2)}, u32[]{:S(2)}) %collective-permute-start.27) | collective-permute-done | bytes 373280 | tf_op jit(solution)/shard_map/ppermute | solution.py:30
  98.5 1.6 %shard_map.30 = f32[27,6912]{1,0:T(8,128)} custom-call(f32[56,3456]{1,0:T(8,128)S(1)} %concatenate.7.mine, f32[27,3456]{1,0:T(8,128)S(1)} %collective-permute-done.27.theirs, f32[27,6912]{1,0:T(8,128)S(1)} %copy-done.1), custom_call_target="tpu_custom_call" | custom-call | bytes 4194304 | tf_op jit(solution)/shard_map/pallas_call | solution.py:202
  (100 shorter events, 8.0 us)
Async XLA Ops:
  0.0 15.6 %collective-permute-start.1 = (bf16[432,512]{1,0:T(8,128)(2,1)}, bf16[432,512]{1,0:T(8,128)(2,1)S(1)}, u32[]{:S(2)}, u32[]{:S(2)}) collective-permute-start(bf16[432,512]{1,0:T(8,128)(2,1)} %bitcast.109), channel_id=1, source_target_pairs={{0,14},{1,15},{2,0},{3,1},{4,2},{5,3},{6,4},{7,5},{8,6},{9,7},{10,... | collective-permute-start | bytes 1327112 | tf_op jit(solution)/shard_map/ppermute | solution.py:30
  6.4 12.5 %collective-permute-start = (bf16[432,512]{1,0:T(8,128)(2,1)}, bf16[432,512]{1,0:T(8,128)(2,1)S(1)}, u32[]{:S(2)}, u32[]{:S(2)}) collective-permute-start(bf16[432,512]{1,0:T(8,128)(2,1)} %bitcast.110), channel_id=1, source_target_pairs={{0,16},{1,17},{2,18},{3,19},{4,20},{5,21},{6,22},{7,23},{8,24},{9,... | collective-permute-start | bytes 1327112 | tf_op jit(solution)/shard_map/ppermute | solution.py:30
  7.4 13.2 %collective-permute-start.3 = (bf16[432,512]{1,0:T(8,128)(2,1)}, bf16[432,512]{1,0:T(8,128)(2,1)S(1)}, u32[]{:S(2)}, u32[]{:S(2)}) collective-permute-start(bf16[432,512]{1,0:T(8,128)(2,1)} %bitcast.111), channel_id=1, source_target_pairs={{0,2},{1,3},{2,4},{3,5},{4,6},{5,7},{6,8},{7,9},{8,10},{9,11},{10,... | collective-permute-start | bytes 1327112 | tf_op jit(solution)/shard_map/ppermute | solution.py:30
  7.4 14.0 %collective-permute-start.5 = (bf16[432,512]{1,0:T(8,128)(2,1)}, bf16[432,512]{1,0:T(8,128)(2,1)S(1)}, u32[]{:S(2)}, u32[]{:S(2)}) collective-permute-start(bf16[432,512]{1,0:T(8,128)(2,1)} %bitcast.112), channel_id=1, source_target_pairs={{0,1},{1,0},{2,3},{3,2},{4,5},{5,4},{6,7},{7,6},{8,9},{9,8},{10,11... | collective-permute-start | bytes 1327112 | tf_op jit(solution)/shard_map/ppermute | solution.py:30
  15.6 11.2 %collective-permute-start.7 = (bf16[432,512]{1,0:T(8,128)(2,1)S(1)}, bf16[432,512]{1,0:T(8,128)(2,1)S(1)}, u32[]{:S(2)}, u32[]{:S(2)}) collective-permute-start(bf16[432,512]{1,0:T(8,128)(2,1)S(1)} %collective-permute-done.1.refs_2_), channel_id=1, source_target_pairs={{0,14},{1,15},{2,0},{3,1},{4,2},{5,3},{6,4},{7,5},{8,6},{9,7},{10,... | collective-permute-start | bytes 1327112 | tf_op jit(solution)/shard_map/ppermute | solution.py:30
  20.6 8.7 %collective-permute-start.4 = (bf16[432,512]{1,0:T(8,128)(2,1)S(1)}, bf16[432,512]{1,0:T(8,128)(2,1)S(1)}, u32[]{:S(2)}, u32[]{:S(2)}) collective-permute-start(bf16[432,512]{1,0:T(8,128)(2,1)S(1)} %collective-permute-done.3.refs_4_.refs_2_), channel_id=1, source_target_pairs={{0,16},{1,17},{2,18},{3,19},{4,20},{5,21},{6,22},{7,23},{8,24},{9,... | collective-permute-start | bytes 1327112 | tf_op jit(solution)/shard_map/ppermute | solution.py:30
  21.4 9.2 %collective-permute-start.2 = (bf16[432,512]{1,0:T(8,128)(2,1)S(1)}, bf16[432,512]{1,0:T(8,128)(2,1)S(1)}, u32[]{:S(2)}, u32[]{:S(2)}) collective-permute-start(bf16[432,512]{1,0:T(8,128)(2,1)S(1)} %collective-permute-done.1.refs_2_), channel_id=1, source_target_pairs={{0,16},{1,17},{2,18},{3,19},{4,20},{5,21},{6,22},{7,23},{8,24},{9,... | collective-permute-start | bytes 1327112 | tf_op jit(solution)/shard_map/ppermute | solution.py:30
  21.4 9.2 %collective-permute-start.6 = (bf16[432,512]{1,0:T(8,128)(2,1)S(1)}, bf16[432,512]{1,0:T(8,128)(2,1)}, u32[]{:S(2)}, u32[]{:S(2)}) collective-permute-start(bf16[432,512]{1,0:T(8,128)(2,1)S(1)} %collective-permute-done.5.refs_6_), channel_id=1, source_target_pairs={{0,16},{1,17},{2,18},{3,19},{4,20},{5,21},{6,22},{7,23},{8,24},{9,... | collective-permute-start | bytes 1327112 | tf_op jit(solution)/shard_map/ppermute | solution.py:30
  26.8 3.9 %collective-permute-start.8 = (bf16[432,512]{1,0:T(8,128)(2,1)S(1)}, bf16[432,512]{1,0:T(8,128)(2,1)S(1)}, u32[]{:S(2)}, u32[]{:S(2)}) collective-permute-start(bf16[432,512]{1,0:T(8,128)(2,1)S(1)} %collective-permute-done.7.refs_8_), channel_id=1, source_target_pairs={{0,16},{1,17},{2,18},{3,19},{4,20},{5,21},{6,22},{7,23},{8,24},{9,... | collective-permute-start | bytes 1327112 | tf_op jit(solution)/shard_map/ppermute | solution.py:30
  29.3 18.8 %collective-permute-start.15 = (bf16[432,512]{1,0:T(8,128)(2,1)S(1)}, bf16[432,512]{1,0:T(8,128)(2,1)S(1)}, u32[]{:S(2)}, u32[]{:S(2)}) collective-permute-start(bf16[432,512]{1,0:T(8,128)(2,1)S(1)} %collective-permute-done.3.refs_4_.refs_2_), channel_id=1, source_target_pairs={{0,2},{1,3},{2,4},{3,5},{4,6},{5,7},{6,8},{7,9},{8,10},{9,11},{10,... | collective-permute-start | bytes 1327112 | tf_op jit(solution)/shard_map/ppermute | solution.py:30
  29.3 11.9 %collective-permute-start.17 = (bf16[432,512]{1,0:T(8,128)(2,1)S(1)}, bf16[432,512]{1,0:T(8,128)(2,1)S(1)}, u32[]{:S(2)}, u32[]{:S(2)}) collective-permute-start(bf16[432,512]{1,0:T(8,128)(2,1)S(1)} %collective-permute-done.7.refs_8_), channel_id=1, source_target_pairs={{0,1},{1,0},{2,3},{3,2},{4,5},{5,4},{6,7},{7,6},{8,9},{9,8},{10,11... | collective-permute-start | bytes 1327112 | tf_op jit(solution)/shard_map/ppermute | solution.py:30
  30.7 1.0 %copy-start = (bf16[512,432]{0,1:T(8,128)(2,1)S(1)}, bf16[512,432]{0,1:T(8,128)(2,1)}, u32[]{:S(2)}) copy-start(bf16[512,432]{0,1:T(8,128)(2,1)} %param.2) | copy-start | bytes 1327108
  36.7 7.7 %collective-permute-start.10 = (f16[56,2160]{1,0:T(8,128)(2,1)S(1)}, f16[56,2160]{1,0:T(8,128)(2,1)S(1)}, u32[]{:S(2)}, u32[]{:S(2)}) collective-permute-start(f16[56,2160]{1,0:T(8,128)(2,1)S(1)} %get-tuple-element.49), channel_id=1, source_target_pairs={{0,192},{1,193},{2,194},{3,195},{4,196},{5,197},{6,198},{7,199},{8... | collective-permute-start | bytes 725768 | tf_op jit(solution)/shard_map/ppermute | solution.py:30
  39.5 8.0 %collective-permute-start.9 = (f16[56,2160]{1,0:T(8,128)(2,1)S(1)}, f16[56,2160]{1,0:T(8,128)(2,1)S(1)}, u32[]{:S(2)}, u32[]{:S(2)}) collective-permute-start(f16[56,2160]{1,0:T(8,128)(2,1)S(1)} %get-tuple-element.50), channel_id=1, source_target_pairs={{0,64},{1,65},{2,66},{3,67},{4,68},{5,69},{6,70},{7,71},{8,72},{9,... | collective-permute-start | bytes 725768 | tf_op jit(solution)/shard_map/ppermute | solution.py:30
  41.1 11.7 %collective-permute-start.18 = (bf16[432,512]{1,0:T(8,128)(2,1)S(1)}, bf16[432,512]{1,0:T(8,128)(2,1)S(1)}, u32[]{:S(2)}, u32[]{:S(2)}) collective-permute-start(bf16[432,512]{1,0:T(8,128)(2,1)S(1)} %collective-permute-done.17.refs_6_), channel_id=1, source_target_pairs={{0,16},{1,17},{2,18},{3,19},{4,20},{5,21},{6,22},{7,23},{8,24},{9,... | collective-permute-start | bytes 1327112 | tf_op jit(solution)/shard_map/ppermute | solution.py:30
  48.1 4.7 %collective-permute-start.16 = (bf16[432,512]{1,0:T(8,128)(2,1)S(1)}, bf16[432,512]{1,0:T(8,128)(2,1)S(1)}, u32[]{:S(2)}, u32[]{:S(2)}) collective-permute-start(bf16[432,512]{1,0:T(8,128)(2,1)S(1)} %collective-permute-done.15.refs_4_), channel_id=1, source_target_pairs={{0,16},{1,17},{2,18},{3,19},{4,20},{5,21},{6,22},{7,23},{8,24},{9,... | collective-permute-start | bytes 1327112 | tf_op jit(solution)/shard_map/ppermute | solution.py:30
  50.1 14.0 %collective-permute-start.11 = (f16[2,56,2160]{2,1,0:T(8,128)(2,1)S(1)}, f16[2,56,2160]{2,1,0:T(8,128)(2,1)S(1)}, u32[]{:S(2)}, u32[]{:S(2)}) collective-permute-start(f16[2,56,2160]{2,1,0:T(8,128)(2,1)S(1)} %get-tuple-element.68), channel_id=1, source_target_pairs={{0,64},{1,65},{2,66},{3,67},{4,68},{5,69},{6,70},{7,71},{8,72},{9,... | collective-permute-start | bytes 1451528 | tf_op jit(solution)/shard_map/ppermute | solution.py:30
  50.2 14.0 %collective-permute-start.12 = (f16[2,56,2160]{2,1,0:T(8,128)(2,1)S(1)}, f16[2,56,2160]{2,1,0:T(8,128)(2,1)S(1)}, u32[]{:S(2)}, u32[]{:S(2)}) collective-permute-start(f16[2,56,2160]{2,1,0:T(8,128)(2,1)S(1)} %get-tuple-element.67), channel_id=1, source_target_pairs={{0,192},{1,193},{2,194},{3,195},{4,196},{5,197},{6,198},{7,199},{8... | collective-permute-start | bytes 1451528 | tf_op jit(solution)/shard_map/ppermute | solution.py:30
  55.8 12.4 %collective-permute-start.19 = (f16[56,1296]{1,0:T(8,128)(2,1)S(1)}, f16[56,1296]{1,0:T(8,128)(2,1)S(1)}, u32[]{:S(2)}, u32[]{:S(2)}) collective-permute-start(f16[56,1296]{1,0:T(8,128)(2,1)S(1)} %get-tuple-element.56), channel_id=1, source_target_pairs={{255,63},{254,62},{253,61},{252,60},{251,59},{250,58},{249,57},{24... | collective-permute-start | bytes 435464 | tf_op jit(solution)/shard_map/ppermute | solution.py:30
  55.8 12.3 %collective-permute-start.20 = (f16[56,1296]{1,0:T(8,128)(2,1)S(1)}, f16[56,1296]{1,0:T(8,128)(2,1)S(1)}, u32[]{:S(2)}, u32[]{:S(2)}) collective-permute-start(f16[56,1296]{1,0:T(8,128)(2,1)S(1)} %get-tuple-element.55), channel_id=1, source_target_pairs={{255,191},{254,190},{253,189},{252,188},{251,187},{250,186},{249,1... | collective-permute-start | bytes 435464 | tf_op jit(solution)/shard_map/ppermute | solution.py:30
  65.1 8.0 %collective-permute-start.13 = (f16[56,2160]{1,0:T(8,128)(2,1)S(1)}, f16[56,2160]{1,0:T(8,128)(2,1)S(1)}, u32[]{:S(2)}, u32[]{:S(2)}) collective-permute-start(f16[56,2160]{1,0:T(8,128)(2,1)S(1)} %fusion.10), channel_id=1, source_target_pairs={{0,32},{1,33},{2,34},{3,35},{4,36},{5,37},{6,38},{7,39},{8,40},{9,... | collective-permute-start | bytes 725768 | tf_op jit(solution)/shard_map/ppermute | solution.py:30
  68.9 8.7 %collective-permute-start.21 = (f16[2,56,1296]{2,1,0:T(8,128)(2,1)S(1)}, f16[2,56,1296]{2,1,0:T(8,128)(2,1)S(1)}, u32[]{:S(2)}, u32[]{:S(2)}) collective-permute-start(f16[2,56,1296]{2,1,0:T(8,128)(2,1)S(1)} %get-tuple-element.66), channel_id=1, source_target_pairs={{255,63},{254,62},{253,61},{252,60},{251,59},{250,58},{249,57},{24... | collective-permute-start | bytes 870920 | tf_op jit(solution)/shard_map/ppermute | solution.py:30
  68.9 8.6 %collective-permute-start.22 = (f16[2,56,1296]{2,1,0:T(8,128)(2,1)S(1)}, f16[2,56,1296]{2,1,0:T(8,128)(2,1)S(1)}, u32[]{:S(2)}, u32[]{:S(2)}) collective-permute-start(f16[2,56,1296]{2,1,0:T(8,128)(2,1)S(1)} %get-tuple-element.65), channel_id=1, source_target_pairs={{255,191},{254,190},{253,189},{252,188},{251,187},{250,186},{249,1... | collective-permute-start | bytes 870920 | tf_op jit(solution)/shard_map/ppermute | solution.py:30
  78.2 20.3 %copy-start.1 = (f32[27,6912]{1,0:T(8,128)S(1)}, f32[27,6912]{1,0:T(8,128)}, u32[]{:S(2)}) copy-start(f32[27,6912]{1,0:T(8,128)} %previous.1) | copy-start | bytes 2239492
  78.8 15.5 %collective-permute-start.23 = (f16[56,1296]{1,0:T(8,128)(2,1)S(1)}, f16[56,1296]{1,0:T(8,128)(2,1)S(1)}, u32[]{:S(2)}, u32[]{:S(2)}) collective-permute-start(f16[56,1296]{1,0:T(8,128)(2,1)S(1)} %pad_maximum_fusion.4), channel_id=1, source_target_pairs={{0,14},{1,15},{2,0},{3,1},{4,2},{5,3},{6,4},{7,5},{8,6},{9,7},{10,... | collective-permute-start | bytes 435464 | tf_op jit(solution)/shard_map/ppermute | solution.py:30
  81.2 13.1 %collective-permute-start.25 = (f16[56,864]{1,0:T(8,128)(2,1)S(1)}, f16[56,864]{1,0:T(8,128)(2,1)S(1)}, u32[]{:S(2)}, u32[]{:S(2)}) collective-permute-start(f16[56,864]{1,0:T(8,128)(2,1)S(1)} %slice.255), channel_id=1, source_target_pairs={{0,12},{1,13},{2,14},{3,15},{4,0},{5,1},{6,2},{7,3},{8,4},{9,5},{1... | collective-permute-start | bytes 290312 | tf_op jit(solution)/shard_map/ppermute | solution.py:30
  82.0 12.3 %collective-permute-start.26 = (f16[56,864]{1,0:T(8,128)(2,1)S(1)}, f16[56,864]{1,0:T(8,128)(2,1)S(1)}, u32[]{:S(2)}, u32[]{:S(2)}) collective-permute-start(f16[56,864]{1,0:T(8,128)(2,1)S(1)} %slice.256), channel_id=1, source_target_pairs={{0,44},{1,45},{2,46},{3,47},{4,32},{5,33},{6,34},{7,35},{8,36},{9,... | collective-permute-start | bytes 290312 | tf_op jit(solution)/shard_map/ppermute | solution.py:30
  87.9 6.4 %collective-permute-start.24 = (f16[56,432]{1,0:T(8,128)(2,1)S(1)}, f16[56,432]{1,0:T(8,128)(2,1)S(1)}, u32[]{:S(2)}, u32[]{:S(2)}) collective-permute-start(f16[56,432]{1,0:T(8,128)(2,1)S(1)} %slice.254), channel_id=1, source_target_pairs={{0,46},{1,47},{2,32},{3,33},{4,34},{5,35},{6,36},{7,37},{8,38},{9,... | collective-permute-start | bytes 145160 | tf_op jit(solution)/shard_map/ppermute | solution.py:30
  88.1 6.7 %collective-permute-start.14 = (f32[56,432]{1,0:T(8,128)S(1)}, f32[56,432]{1,0:T(8,128)S(1)}, u32[]{:S(2)}, u32[]{:S(2)}) collective-permute-start(f32[56,432]{1,0:T(8,128)S(1)} %get-tuple-element.61), channel_id=1, source_target_pairs={{0,1},{1,0},{2,3},{3,2},{4,5},{5,4},{6,7},{7,6},{8,9},{9,8},{10,11... | collective-permute-start | bytes 290312 | tf_op jit(solution)/shard_map/ppermute | solution.py:30
  95.3 3.2 %collective-permute-start.27 = (f32[27,3456]{1,0:T(8,128)S(1)}, f32[27,3456]{1,0:T(8,128)S(1)}, u32[]{:S(2)}, u32[]{:S(2)}) collective-permute-start(f32[27,3456]{1,0:T(8,128)S(1)} %constant_dynamic-slice_fusion.3), channel_id=1, source_target_pairs={{0,16},{1,17},{2,18},{3,19},{4,20},{5,21},{6,22},{7,23},{8,24},{9,... | collective-permute-start | bytes 1119752 | tf_op jit(solution)/shard_map/ppermute | solution.py:30

commit v3 on v1

--- a/solution.py
+++ b/solution.py
@@ -119,9 +119,12 @@
     return lax.slice_in_dim(value, n_rows, n_rows + 1, axis=value.ndim - 2)
 
 
-def packed(value, n_rows):
+def packed(value, n_rows, flat=False):
     scaled = value * jnp.exp2(-exponent_row(value, n_rows))
-    return jnp.where(at_exponent(value, n_rows), value, scaled).astype(jnp.float16)
+    scaled = jnp.where(at_exponent(value, n_rows), value, scaled)
+    if flat:
+        scaled = scaled.reshape(-1, value.shape[-1])
+    return scaled.astype(jnp.float16)
 
 
 def unpacked(value, n_rows):
@@ -150,12 +153,13 @@
     above, below = chunk_of(part, y_at + 1), chunk_of(part, y_at + 3)
     first = added(above[0], unpacked(arrived[0], n_rows), n_rows)
     second = added(below[1], unpacked(arrived[1], n_rows), n_rows)
-    to_above = packed(jnp.stack([first, above[1]]), n_rows)
-    to_below = packed(jnp.stack([below[0], second]), n_rows)
+    to_above = packed(jnp.stack([first, above[1]]), n_rows, True)
+    to_below = packed(jnp.stack([below[0], second]), n_rows, True)
     return to_above, to_below
 
 
 def y_last(part, arrived, n_rows, y_at):
+    arrived = [value.astype(jnp.float32).reshape(NXH, -1, value.shape[1]) for value in arrived]
     summed = added(unpacked(arrived[0], n_rows), unpacked(arrived[1], n_rows), n_rows)
     return added(chunk_of(part, y_at), summed, n_rows)
 

time: 96.2 us -> 96.8 us (level)
  transfers between devices with their start and end apart: 28 -> 28, of which waited for: 13 -> 12; matrix products, arithmetic and copies ran while one was open for 5% -> 6% of each run, Pallas kernels for 8% -> 8%
where the time goes in v3:
time: 96.8 us; the launch traced here: 96.6 us
  starting transfers between devices  44.6 us (46%)
  waiting for transfers between devices  35.5 us (37%)
  Pallas kernels  8.95 us (9%)
  other arithmetic  4.87 us (5%)
  local copies, waits for them, and re-layouts  2.06 us (2%)
    ppermute x28, starting transfers between devices, move(): return lax.ppermute(value, AXES, pairs[::-1] if turned else pairs)  44.6 us
    ppermute x28, waiting for transfers between devices, move(): return lax.ppermute(value, AXES, pairs[::-1] if turned else pairs)  35.5 us
    pallas_call x2, Pallas kernels, products(): pl.pallas_call(functools.partial(products_kernel, units, len(shards), wid...  7.4 us
  transfers between devices with their start and end apart: 28, of which 12 were waited for; matrix products, arithmetic and copies ran while one was open for 6% of the time, Pallas kernels for 8%

profile of v3, /device:TPU:1, one launch (start us, length us, event | category | flops | bytes accessed | tf_op | source)
XLA Modules:
  0.0 96.6 jit_solution(7677200552439166846)
XLA Ops:
  0.0 6.4 %collective-permute-start.1 = (bf16[432,512]{1,0:T(8,128)(2,1)}, bf16[432,512]{1,0:T(8,128)(2,1)S(1)}, u32[]{:S(2)}, u32[]{:S(2)}) collective-permute-start(bf16[432,512]{1,0:T(8,128)(2,1)} %bitcast.133), channel_id=1, source_target_pairs={{0,14},{1,15},{2,0},{3,1},{4,2},{5,3},{6,4},{7,5},{8,6},{9,7},{10,... | collective-permute-start | bytes 1327112 | tf_op jit(solution)/shard_map/ppermute | solution.py:30
  6.4 1.0 collective-permute-start
  7.4 1.2 %collective-permute-start.5 = (bf16[432,512]{1,0:T(8,128)(2,1)}, bf16[432,512]{1,0:T(8,128)(2,1)S(1)}, u32[]{:S(2)}, u32[]{:S(2)}) collective-permute-start(bf16[432,512]{1,0:T(8,128)(2,1)} %bitcast.136), channel_id=1, source_target_pairs={{0,1},{1,0},{2,3},{3,2},{4,5},{5,4},{6,7},{7,6},{8,9},{9,8},{10,11... | collective-permute-start | bytes 1327112 | tf_op jit(solution)/shard_map/ppermute | solution.py:30
  8.6 7.0 %collective-permute-done.1.refs_2_ = bf16[432,512]{1,0:T(8,128)(2,1)S(1)} collective-permute-done((bf16[432,512]{1,0:T(8,128)(2,1)}, bf16[432,512]{1,0:T(8,128)(2,1)S(1)}, u32[]{:S(2)}, u32[]{:S(2)}) %collective-permute-start.1) | collective-permute-done | bytes 442400 | tf_op jit(solution)/shard_map/ppermute | solution.py:30
  15.6 3.3 %collective-permute-start.7 = (bf16[432,512]{1,0:T(8,128)(2,1)S(1)}, bf16[432,512]{1,0:T(8,128)(2,1)S(1)}, u32[]{:S(2)}, u32[]{:S(2)}) collective-permute-start(bf16[432,512]{1,0:T(8,128)(2,1)S(1)} %collective-permute-done.1.refs_2_), channel_id=1, source_target_pairs={{0,14},{1,15},{2,0},{3,1},{4,2},{5,3},{6,4},{7,5},{8,6},{9,7},{10,... | collective-permute-start | bytes 1327112 | tf_op jit(solution)/shard_map/ppermute | solution.py:30
  18.9 1.7 %collective-permute-done.3.refs_4_.refs_2_ = bf16[432,512]{1,0:T(8,128)(2,1)S(1)} collective-permute-done((bf16[432,512]{1,0:T(8,128)(2,1)}, bf16[432,512]{1,0:T(8,128)(2,1)S(1)}, u32[]{:S(2)}, u32[]{:S(2)}) %collective-permute-start.3) | collective-permute-done | bytes 442400 | tf_op jit(solution)/shard_map/ppermute | solution.py:30
  20.6 0.8 collective-permute-start.4
  21.9 4.9 %collective-permute-done.7.refs_8_ = bf16[432,512]{1,0:T(8,128)(2,1)S(1)} collective-permute-done((bf16[432,512]{1,0:T(8,128)(2,1)S(1)}, bf16[432,512]{1,0:T(8,128)(2,1)S(1)}, u32[]{:S(2)}, u32[]{:S(2)}) %collective-permute-start.7) | collective-permute-done | bytes 442400 | tf_op jit(solution)/shard_map/ppermute | solution.py:30
  26.8 2.5 %collective-permute-start.8 = (bf16[432,512]{1,0:T(8,128)(2,1)S(1)}, bf16[432,512]{1,0:T(8,128)(2,1)S(1)}, u32[]{:S(2)}, u32[]{:S(2)}) collective-permute-start(bf16[432,512]{1,0:T(8,128)(2,1)S(1)} %collective-permute-done.7.refs_8_), channel_id=1, source_target_pairs={{0,16},{1,17},{2,18},{3,19},{4,20},{5,21},{6,22},{7,23},{8,24},{9,... | collective-permute-start | bytes 1327112 | tf_op jit(solution)/shard_map/ppermute | solution.py:30
  29.4 1.3 %collective-permute-start.17 = (bf16[432,512]{1,0:T(8,128)(2,1)S(1)}, bf16[432,512]{1,0:T(8,128)(2,1)S(1)}, u32[]{:S(2)}, u32[]{:S(2)}) collective-permute-start(bf16[432,512]{1,0:T(8,128)(2,1)S(1)} %collective-permute-done.7.refs_8_), channel_id=1, source_target_pairs={{0,1},{1,0},{2,3},{3,2},{4,5},{5,4},{6,7},{7,6},{8,9},{9,8},{10,11... | collective-permute-start | bytes 1327112 | tf_op jit(solution)/shard_map/ppermute | solution.py:30
  30.7 1.0 %copy-done = bf16[512,432]{0,1:T(8,128)(2,1)S(1)} copy-done((bf16[512,432]{0,1:T(8,128)(2,1)S(1)}, bf16[512,432]{0,1:T(8,128)(2,1)}, u32[]{:S(2)}) %copy-start) | copy-done | bytes 442392
  31.7 4.7 %shard_map.28 = f32[4,2,56,2160]{3,2,1,0:T(8,128)S(1)} custom-call(bf16[432,512]{1,0:T(8,128)(2,1)S(1)} %bitcast.137, bf16[432,512]{1,0:T(8,128)(2,1)S(1)} %collective-permute-done.refs_1_, bf16[432,512]{1,0:T(8,128)(2,1)S(1)} %collective-permute-done.1.refs_2_, bf16[432,512]{1,0:T(8,128)(2,1)S(1)} %collective-permute-done.2.refs_3_, ...), custom_call_target="tpu_custom_call" | custom-call | flops 1911029760 | bytes 8388608 | tf_op jit(solution)/shard_map/pallas_call | solution.py:97
  36.7 2.8 %collective-permute-start.10 = (f16[56,2160]{1,0:T(8,128)(2,1)S(1)}, f16[56,2160]{1,0:T(8,128)(2,1)S(1)}, u32[]{:S(2)}, u32[]{:S(2)}) collective-permute-start(f16[56,2160]{1,0:T(8,128)(2,1)S(1)} %get-tuple-element.49), channel_id=1, source_target_pairs={{0,192},{1,193},{2,194},{3,195},{4,196},{5,197},{6,198},{7,199},{8... | collective-permute-start | bytes 725768 | tf_op jit(solution)/shard_map/ppermute | solution.py:30
  39.6 1.7 %collective-permute-done.17.refs_6_ = bf16[432,512]{1,0:T(8,128)(2,1)S(1)} collective-permute-done((bf16[432,512]{1,0:T(8,128)(2,1)S(1)}, bf16[432,512]{1,0:T(8,128)(2,1)S(1)}, u32[]{:S(2)}, u32[]{:S(2)}) %collective-permute-start.17) | collective-permute-done | bytes 442400 | tf_op jit(solution)/shard_map/ppermute | solution.py:30
  41.3 0.8 collective-permute-start.18
  42.1 1.3 %collective-permute-done.15.refs_4_ = bf16[432,512]{1,0:T(8,128)(2,1)S(1)} collective-permute-done((bf16[432,512]{1,0:T(8,128)(2,1)S(1)}, bf16[432,512]{1,0:T(8,128)(2,1)S(1)}, u32[]{:S(2)}, u32[]{:S(2)}) %collective-permute-start.15) | collective-permute-done | bytes 442400 | tf_op jit(solution)/shard_map/ppermute | solution.py:30
  44.5 3.1 %collective-permute-done.9 = f16[56,2160]{1,0:T(8,128)(2,1)S(1)} collective-permute-done((f16[56,2160]{1,0:T(8,128)(2,1)S(1)}, f16[56,2160]{1,0:T(8,128)(2,1)S(1)}, u32[]{:S(2)}, u32[]{:S(2)}) %collective-permute-start.9) | collective-permute-done | bytes 241952 | tf_op jit(solution)/shard_map/ppermute | solution.py:30
  48.8 2.7 %collective-permute-start.12 = (f16[112,2160]{1,0:T(8,128)(2,1)S(1)}, f16[112,2160]{1,0:T(8,128)(2,1)S(1)}, u32[]{:S(2)}, u32[]{:S(2)}) collective-permute-start(f16[112,2160]{1,0:T(8,128)(2,1)S(1)} %get-tuple-element.67), channel_id=1, source_target_pairs={{0,192},{1,193},{2,194},{3,195},{4,196},{5,197},{6,198},{7,199},{8... | collective-permute-start | bytes 1451528 | tf_op jit(solution)/shard_map/ppermute | solution.py:30
  51.5 2.7 %shard_map.29 = f32[4,2,56,1296]{3,2,1,0:T(8,128)S(1)} custom-call(bf16[432,512]{1,0:T(8,128)(2,1)S(1)} %bitcast.138, bf16[432,512]{1,0:T(8,128)(2,1)S(1)} %collective-permute-done.refs_1_, bf16[432,512]{1,0:T(8,128)(2,1)S(1)} %collective-permute-done.3.refs_4_.refs_2_, bf16[432,512]{1,0:T(8,128)(2,1)S(1)} %collective-permute-done.4.refs_5_.refs_3_, ...), custom_call_target="tpu_custom_call" | custom-call | flops 1146617856 | bytes 8388608 | tf_op jit(solution)/shard_map/pallas_call | solution.py:97
  54.5 2.7 %collective-permute-start.20 = (f16[56,1296]{1,0:T(8,128)(2,1)S(1)}, f16[56,1296]{1,0:T(8,128)(2,1)S(1)}, u32[]{:S(2)}, u32[]{:S(2)}) collective-permute-start(f16[56,1296]{1,0:T(8,128)(2,1)S(1)} %get-tuple-element.55), channel_id=1, source_target_pairs={{255,191},{254,190},{253,189},{252,188},{251,187},{250,186},{249,1... | collective-permute-start | bytes 435464 | tf_op jit(solution)/shard_map/ppermute | solution.py:30
  57.2 7.3 %collective-permute-done.19 = f16[56,1296]{1,0:T(8,128)(2,1)S(1)} collective-permute-done((f16[56,1296]{1,0:T(8,128)(2,1)S(1)}, f16[56,1296]{1,0:T(8,128)(2,1)S(1)}, u32[]{:S(2)}, u32[]{:S(2)}) %collective-permute-start.19) | collective-permute-done | bytes 145184 | tf_op jit(solution)/shard_map/ppermute | solution.py:30
  65.7 2.7 %collective-permute-start.22 = (f16[112,1296]{1,0:T(8,128)(2,1)S(1)}, f16[112,1296]{1,0:T(8,128)(2,1)S(1)}, u32[]{:S(2)}, u32[]{:S(2)}) collective-permute-start(f16[112,1296]{1,0:T(8,128)(2,1)S(1)} %get-tuple-element.65), channel_id=1, source_target_pairs={{255,191},{254,190},{253,189},{252,188},{251,187},{250,186},{249,1... | collective-permute-start | bytes 870920 | tf_op jit(solution)/shard_map/ppermute | solution.py:30
  69.3 2.6 %collective-permute-start.13 = (f16[56,2160]{1,0:T(8,128)(2,1)S(1)}, f16[56,2160]{1,0:T(8,128)(2,1)S(1)}, u32[]{:S(2)}, u32[]{:S(2)}) collective-permute-start(f16[56,2160]{1,0:T(8,128)(2,1)S(1)} %fusion.10), channel_id=1, source_target_pairs={{0,32},{1,33},{2,34},{3,35},{4,36},{5,37},{6,38},{7,39},{8,40},{9,... | collective-permute-start | bytes 725768 | tf_op jit(solution)/shard_map/ppermute | solution.py:30
  71.9 1.5 %collective-permute-done.21 = f16[112,1296]{1,0:T(8,128)(2,1)S(1)} collective-permute-done((f16[112,1296]{1,0:T(8,128)(2,1)S(1)}, f16[112,1296]{1,0:T(8,128)(2,1)S(1)}, u32[]{:S(2)}, u32[]{:S(2)}) %collective-permute-start.21) | collective-permute-done | bytes 290336 | tf_op jit(solution)/shard_map/ppermute | solution.py:30
  74.5 1.9 %collective-permute-start.25 = (f16[56,864]{1,0:T(8,128)(2,1)S(1)}, f16[56,864]{1,0:T(8,128)(2,1)S(1)}, u32[]{:S(2)}, u32[]{:S(2)}) collective-permute-start(f16[56,864]{1,0:T(8,128)(2,1)S(1)} %slice.255), channel_id=1, source_target_pairs={{0,12},{1,13},{2,14},{3,15},{4,0},{5,1},{6,2},{7,3},{8,4},{9,5},{1... | collective-permute-start | bytes 290312 | tf_op jit(solution)/shard_map/ppermute | solution.py:30
  76.4 2.7 %collective-permute-start.26 = (f16[56,864]{1,0:T(8,128)(2,1)S(1)}, f16[56,864]{1,0:T(8,128)(2,1)S(1)}, u32[]{:S(2)}, u32[]{:S(2)}) collective-permute-start(f16[56,864]{1,0:T(8,128)(2,1)S(1)} %slice.256), channel_id=1, source_target_pairs={{0,44},{1,45},{2,46},{3,47},{4,32},{5,33},{6,34},{7,35},{8,36},{9,... | collective-permute-start | bytes 290312 | tf_op jit(solution)/shard_map/ppermute | solution.py:30
  80.3 3.7 %collective-permute-start.23 = (f16[56,1296]{1,0:T(8,128)(2,1)S(1)}, f16[56,1296]{1,0:T(8,128)(2,1)S(1)}, u32[]{:S(2)}, u32[]{:S(2)}) collective-permute-start(f16[56,1296]{1,0:T(8,128)(2,1)S(1)} %pad_maximum_fusion.4), channel_id=1, source_target_pairs={{0,14},{1,15},{2,0},{3,1},{4,2},{5,3},{6,4},{7,5},{8,6},{9,7},{10,... | collective-permute-start | bytes 435464 | tf_op jit(solution)/shard_map/ppermute | solution.py:30
  84.1 1.0 %collective-permute-start.14 = (f32[56,432]{1,0:T(8,128)S(1)}, f32[56,432]{1,0:T(8,128)S(1)}, u32[]{:S(2)}, u32[]{:S(2)}) collective-permute-start(f32[56,432]{1,0:T(8,128)S(1)} %get-tuple-element.61), channel_id=1, source_target_pairs={{0,1},{1,0},{2,3},{3,2},{4,5},{5,4},{6,7},{7,6},{8,9},{9,8},{10,11... | collective-permute-start | bytes 290312 | tf_op jit(solution)/shard_map/ppermute | solution.py:30
  85.2 4.3 %collective-permute-done.23 = f16[56,1296]{1,0:T(8,128)(2,1)S(1)} collective-permute-done((f16[56,1296]{1,0:T(8,128)(2,1)S(1)}, f16[56,1296]{1,0:T(8,128)(2,1)S(1)}, u32[]{:S(2)}, u32[]{:S(2)}) %collective-permute-start.23) | collective-permute-done | bytes 145184 | tf_op jit(solution)/shard_map/ppermute | solution.py:30
  91.1 2.5 %collective-permute-start.27 = (f32[27,3456]{1,0:T(8,128)S(1)}, f32[27,3456]{1,0:T(8,128)S(1)}, u32[]{:S(2)}, u32[]{:S(2)}) collective-permute-start(f32[27,3456]{1,0:T(8,128)S(1)} %constant_dynamic-slice_fusion.3), channel_id=1, source_target_pairs={{0,16},{1,17},{2,18},{3,19},{4,20},{5,21},{6,22},{7,23},{8,24},{9,... | collective-permute-start | bytes 1119752 | tf_op jit(solution)/shard_map/ppermute | solution.py:30
  93.6 1.4 %collective-permute-done.27.theirs = f32[27,3456]{1,0:T(8,128)S(1)} collective-permute-done((f32[27,3456]{1,0:T(8,128)S(1)}, f32[27,3456]{1,0:T(8,128)S(1)}, u32[]{:S(2)}, u32[]{:S(2)}) %collective-permute-start.27) | collective-permute-done | bytes 373280 | tf_op jit(solution)/shard_map/ppermute | solution.py:30
  95.1 1.6 %shard_map.30 = f32[27,6912]{1,0:T(8,128)} custom-call(f32[56,3456]{1,0:T(8,128)S(1)} %concatenate.7.mine, f32[27,3456]{1,0:T(8,128)S(1)} %collective-permute-done.27.theirs, f32[27,6912]{1,0:T(8,128)S(1)} %copy-done.1), custom_call_target="tpu_custom_call" | custom-call | bytes 4194304 | tf_op jit(solution)/shard_map/pallas_call | solution.py:206
  (105 shorter events, 9.3 us)
Async XLA Ops:
  0.0 15.6 %collective-permute-start.1 = (bf16[432,512]{1,0:T(8,128)(2,1)}, bf16[432,512]{1,0:T(8,128)(2,1)S(1)}, u32[]{:S(2)}, u32[]{:S(2)}) collective-permute-start(bf16[432,512]{1,0:T(8,128)(2,1)} %bitcast.133), channel_id=1, source_target_pairs={{0,14},{1,15},{2,0},{3,1},{4,2},{5,3},{6,4},{7,5},{8,6},{9,7},{10,... | collective-permute-start | bytes 1327112 | tf_op jit(solution)/shard_map/ppermute | solution.py:30
  6.4 12.5 %collective-permute-start = (bf16[432,512]{1,0:T(8,128)(2,1)}, bf16[432,512]{1,0:T(8,128)(2,1)S(1)}, u32[]{:S(2)}, u32[]{:S(2)}) collective-permute-start(bf16[432,512]{1,0:T(8,128)(2,1)} %bitcast.134), channel_id=1, source_target_pairs={{0,16},{1,17},{2,18},{3,19},{4,20},{5,21},{6,22},{7,23},{8,24},{9,... | collective-permute-start | bytes 1327112 | tf_op jit(solution)/shard_map/ppermute | solution.py:30
  7.4 13.2 %collective-permute-start.3 = (bf16[432,512]{1,0:T(8,128)(2,1)}, bf16[432,512]{1,0:T(8,128)(2,1)S(1)}, u32[]{:S(2)}, u32[]{:S(2)}) collective-permute-start(bf16[432,512]{1,0:T(8,128)(2,1)} %bitcast.135), channel_id=1, source_target_pairs={{0,2},{1,3},{2,4},{3,5},{4,6},{5,7},{6,8},{7,9},{8,10},{9,11},{10,... | collective-permute-start | bytes 1327112 | tf_op jit(solution)/shard_map/ppermute | solution.py:30
  7.4 14.0 %collective-permute-start.5 = (bf16[432,512]{1,0:T(8,128)(2,1)}, bf16[432,512]{1,0:T(8,128)(2,1)S(1)}, u32[]{:S(2)}, u32[]{:S(2)}) collective-permute-start(bf16[432,512]{1,0:T(8,128)(2,1)} %bitcast.136), channel_id=1, source_target_pairs={{0,1},{1,0},{2,3},{3,2},{4,5},{5,4},{6,7},{7,6},{8,9},{9,8},{10,11... | collective-permute-start | bytes 1327112 | tf_op jit(solution)/shard_map/ppermute | solution.py:30
  15.6 11.2 %collective-permute-start.7 = (bf16[432,512]{1,0:T(8,128)(2,1)S(1)}, bf16[432,512]{1,0:T(8,128)(2,1)S(1)}, u32[]{:S(2)}, u32[]{:S(2)}) collective-permute-start(bf16[432,512]{1,0:T(8,128)(2,1)S(1)} %collective-permute-done.1.refs_2_), channel_id=1, source_target_pairs={{0,14},{1,15},{2,0},{3,1},{4,2},{5,3},{6,4},{7,5},{8,6},{9,7},{10,... | collective-permute-start | bytes 1327112 | tf_op jit(solution)/shard_map/ppermute | solution.py:30
  20.6 8.8 %collective-permute-start.4 = (bf16[432,512]{1,0:T(8,128)(2,1)S(1)}, bf16[432,512]{1,0:T(8,128)(2,1)S(1)}, u32[]{:S(2)}, u32[]{:S(2)}) collective-permute-start(bf16[432,512]{1,0:T(8,128)(2,1)S(1)} %collective-permute-done.3.refs_4_.refs_2_), channel_id=1, source_target_pairs={{0,16},{1,17},{2,18},{3,19},{4,20},{5,21},{6,22},{7,23},{8,24},{9,... | collective-permute-start | bytes 1327112 | tf_op jit(solution)/shard_map/ppermute | solution.py:30
  21.4 9.3 %collective-permute-start.2 = (bf16[432,512]{1,0:T(8,128)(2,1)S(1)}, bf16[432,512]{1,0:T(8,128)(2,1)S(1)}, u32[]{:S(2)}, u32[]{:S(2)}) collective-permute-start(bf16[432,512]{1,0:T(8,128)(2,1)S(1)} %collective-permute-done.1.refs_2_), channel_id=1, source_target_pairs={{0,16},{1,17},{2,18},{3,19},{4,20},{5,21},{6,22},{7,23},{8,24},{9,... | collective-permute-start | bytes 1327112 | tf_op jit(solution)/shard_map/ppermute | solution.py:30
  21.4 9.3 %collective-permute-start.6 = (bf16[432,512]{1,0:T(8,128)(2,1)S(1)}, bf16[432,512]{1,0:T(8,128)(2,1)}, u32[]{:S(2)}, u32[]{:S(2)}) collective-permute-start(bf16[432,512]{1,0:T(8,128)(2,1)S(1)} %collective-permute-done.5.refs_6_), channel_id=1, source_target_pairs={{0,16},{1,17},{2,18},{3,19},{4,20},{5,21},{6,22},{7,23},{8,24},{9,... | collective-permute-start | bytes 1327112 | tf_op jit(solution)/shard_map/ppermute | solution.py:30
  26.8 3.9 %collective-permute-start.8 = (bf16[432,512]{1,0:T(8,128)(2,1)S(1)}, bf16[432,512]{1,0:T(8,128)(2,1)S(1)}, u32[]{:S(2)}, u32[]{:S(2)}) collective-permute-start(bf16[432,512]{1,0:T(8,128)(2,1)S(1)} %collective-permute-done.7.refs_8_), channel_id=1, source_target_pairs={{0,16},{1,17},{2,18},{3,19},{4,20},{5,21},{6,22},{7,23},{8,24},{9,... | collective-permute-start | bytes 1327112 | tf_op jit(solution)/shard_map/ppermute | solution.py:30
  29.4 14.0 %collective-permute-start.15 = (bf16[432,512]{1,0:T(8,128)(2,1)S(1)}, bf16[432,512]{1,0:T(8,128)(2,1)S(1)}, u32[]{:S(2)}, u32[]{:S(2)}) collective-permute-start(bf16[432,512]{1,0:T(8,128)(2,1)S(1)} %collective-permute-done.3.refs_4_.refs_2_), channel_id=1, source_target_pairs={{0,2},{1,3},{2,4},{3,5},{4,6},{5,7},{6,8},{7,9},{8,10},{9,11},{10,... | collective-permute-start | bytes 1327112 | tf_op jit(solution)/shard_map/ppermute | solution.py:30
  29.4 11.9 %collective-permute-start.17 = (bf16[432,512]{1,0:T(8,128)(2,1)S(1)}, bf16[432,512]{1,0:T(8,128)(2,1)S(1)}, u32[]{:S(2)}, u32[]{:S(2)}) collective-permute-start(bf16[432,512]{1,0:T(8,128)(2,1)S(1)} %collective-permute-done.7.refs_8_), channel_id=1, source_target_pairs={{0,1},{1,0},{2,3},{3,2},{4,5},{5,4},{6,7},{7,6},{8,9},{9,8},{10,11... | collective-permute-start | bytes 1327112 | tf_op jit(solution)/shard_map/ppermute | solution.py:30
  30.7 1.0 %copy-start = (bf16[512,432]{0,1:T(8,128)(2,1)S(1)}, bf16[512,432]{0,1:T(8,128)(2,1)}, u32[]{:S(2)}) copy-start(bf16[512,432]{0,1:T(8,128)(2,1)} %param.2) | copy-start | bytes 1327108
  36.7 7.8 %collective-permute-start.10 = (f16[56,2160]{1,0:T(8,128)(2,1)S(1)}, f16[56,2160]{1,0:T(8,128)(2,1)S(1)}, u32[]{:S(2)}, u32[]{:S(2)}) collective-permute-start(f16[56,2160]{1,0:T(8,128)(2,1)S(1)} %get-tuple-element.49), channel_id=1, source_target_pairs={{0,192},{1,193},{2,194},{3,195},{4,196},{5,197},{6,198},{7,199},{8... | collective-permute-start | bytes 725768 | tf_op jit(solution)/shard_map/ppermute | solution.py:30
  39.6 8.1 %collective-permute-start.9 = (f16[56,2160]{1,0:T(8,128)(2,1)S(1)}, f16[56,2160]{1,0:T(8,128)(2,1)S(1)}, u32[]{:S(2)}, u32[]{:S(2)}) collective-permute-start(f16[56,2160]{1,0:T(8,128)(2,1)S(1)} %get-tuple-element.50), channel_id=1, source_target_pairs={{0,64},{1,65},{2,66},{3,67},{4,68},{5,69},{6,70},{7,71},{8,72},{9,... | collective-permute-start | bytes 725768 | tf_op jit(solution)/shard_map/ppermute | solution.py:30
  41.3 10.2 %collective-permute-start.18 = (bf16[432,512]{1,0:T(8,128)(2,1)S(1)}, bf16[432,512]{1,0:T(8,128)(2,1)S(1)}, u32[]{:S(2)}, u32[]{:S(2)}) collective-permute-start(bf16[432,512]{1,0:T(8,128)(2,1)S(1)} %collective-permute-done.17.refs_6_), channel_id=1, source_target_pairs={{0,16},{1,17},{2,18},{3,19},{4,20},{5,21},{6,22},{7,23},{8,24},{9,... | collective-permute-start | bytes 1327112 | tf_op jit(solution)/shard_map/ppermute | solution.py:30
  43.3 8.2 %collective-permute-start.16 = (bf16[432,512]{1,0:T(8,128)(2,1)S(1)}, bf16[432,512]{1,0:T(8,128)(2,1)S(1)}, u32[]{:S(2)}, u32[]{:S(2)}) collective-permute-start(bf16[432,512]{1,0:T(8,128)(2,1)S(1)} %collective-permute-done.15.refs_4_), channel_id=1, source_target_pairs={{0,16},{1,17},{2,18},{3,19},{4,20},{5,21},{6,22},{7,23},{8,24},{9,... | collective-permute-start | bytes 1327112 | tf_op jit(solution)/shard_map/ppermute | solution.py:30
  48.7 19.6 %collective-permute-start.11 = (f16[112,2160]{1,0:T(8,128)(2,1)S(1)}, f16[112,2160]{1,0:T(8,128)(2,1)S(1)}, u32[]{:S(2)}, u32[]{:S(2)}) collective-permute-start(f16[112,2160]{1,0:T(8,128)(2,1)S(1)} %get-tuple-element.68), channel_id=1, source_target_pairs={{0,64},{1,65},{2,66},{3,67},{4,68},{5,69},{6,70},{7,71},{8,72},{9,... | collective-permute-start | bytes 1451528 | tf_op jit(solution)/shard_map/ppermute | solution.py:30
  48.8 19.5 %collective-permute-start.12 = (f16[112,2160]{1,0:T(8,128)(2,1)S(1)}, f16[112,2160]{1,0:T(8,128)(2,1)S(1)}, u32[]{:S(2)}, u32[]{:S(2)}) collective-permute-start(f16[112,2160]{1,0:T(8,128)(2,1)S(1)} %get-tuple-element.67), channel_id=1, source_target_pairs={{0,192},{1,193},{2,194},{3,195},{4,196},{5,197},{6,198},{7,199},{8... | collective-permute-start | bytes 1451528 | tf_op jit(solution)/shard_map/ppermute | solution.py:30
  54.4 10.1 %collective-permute-start.19 = (f16[56,1296]{1,0:T(8,128)(2,1)S(1)}, f16[56,1296]{1,0:T(8,128)(2,1)S(1)}, u32[]{:S(2)}, u32[]{:S(2)}) collective-permute-start(f16[56,1296]{1,0:T(8,128)(2,1)S(1)} %get-tuple-element.56), channel_id=1, source_target_pairs={{255,63},{254,62},{253,61},{252,60},{251,59},{250,58},{249,57},{24... | collective-permute-start | bytes 435464 | tf_op jit(solution)/shard_map/ppermute | solution.py:30
  54.5 10.1 %collective-permute-start.20 = (f16[56,1296]{1,0:T(8,128)(2,1)S(1)}, f16[56,1296]{1,0:T(8,128)(2,1)S(1)}, u32[]{:S(2)}, u32[]{:S(2)}) collective-permute-start(f16[56,1296]{1,0:T(8,128)(2,1)S(1)} %get-tuple-element.55), channel_id=1, source_target_pairs={{255,191},{254,190},{253,189},{252,188},{251,187},{250,186},{249,1... | collective-permute-start | bytes 435464 | tf_op jit(solution)/shard_map/ppermute | solution.py:30
  65.4 8.1 %collective-permute-start.21 = (f16[112,1296]{1,0:T(8,128)(2,1)S(1)}, f16[112,1296]{1,0:T(8,128)(2,1)S(1)}, u32[]{:S(2)}, u32[]{:S(2)}) collective-permute-start(f16[112,1296]{1,0:T(8,128)(2,1)S(1)} %get-tuple-element.66), channel_id=1, source_target_pairs={{255,63},{254,62},{253,61},{252,60},{251,59},{250,58},{249,57},{24... | collective-permute-start | bytes 870920 | tf_op jit(solution)/shard_map/ppermute | solution.py:30
  65.7 7.8 %collective-permute-start.22 = (f16[112,1296]{1,0:T(8,128)(2,1)S(1)}, f16[112,1296]{1,0:T(8,128)(2,1)S(1)}, u32[]{:S(2)}, u32[]{:S(2)}) collective-permute-start(f16[112,1296]{1,0:T(8,128)(2,1)S(1)} %get-tuple-element.65), channel_id=1, source_target_pairs={{255,191},{254,190},{253,189},{252,188},{251,187},{250,186},{249,1... | collective-permute-start | bytes 870920 | tf_op jit(solution)/shard_map/ppermute | solution.py:30
  69.3 10.4 %collective-permute-start.13 = (f16[56,2160]{1,0:T(8,128)(2,1)S(1)}, f16[56,2160]{1,0:T(8,128)(2,1)S(1)}, u32[]{:S(2)}, u32[]{:S(2)}) collective-permute-start(f16[56,2160]{1,0:T(8,128)(2,1)S(1)} %fusion.10), channel_id=1, source_target_pairs={{0,32},{1,33},{2,34},{3,35},{4,36},{5,37},{6,38},{7,39},{8,40},{9,... | collective-permute-start | bytes 725768 | tf_op jit(solution)/shard_map/ppermute | solution.py:30
  74.5 10.6 %collective-permute-start.25 = (f16[56,864]{1,0:T(8,128)(2,1)S(1)}, f16[56,864]{1,0:T(8,128)(2,1)S(1)}, u32[]{:S(2)}, u32[]{:S(2)}) collective-permute-start(f16[56,864]{1,0:T(8,128)(2,1)S(1)} %slice.255), channel_id=1, source_target_pairs={{0,12},{1,13},{2,14},{3,15},{4,0},{5,1},{6,2},{7,3},{8,4},{9,5},{1... | collective-permute-start | bytes 290312 | tf_op jit(solution)/shard_map/ppermute | solution.py:30
  76.4 8.7 %collective-permute-start.26 = (f16[56,864]{1,0:T(8,128)(2,1)S(1)}, f16[56,864]{1,0:T(8,128)(2,1)S(1)}, u32[]{:S(2)}, u32[]{:S(2)}) collective-permute-start(f16[56,864]{1,0:T(8,128)(2,1)S(1)} %slice.256), channel_id=1, source_target_pairs={{0,44},{1,45},{2,46},{3,47},{4,32},{5,33},{6,34},{7,35},{8,36},{9,... | collective-permute-start | bytes 290312 | tf_op jit(solution)/shard_map/ppermute | solution.py:30
  79.1 6.0 %collective-permute-start.24 = (f16[56,432]{1,0:T(8,128)(2,1)S(1)}, f16[56,432]{1,0:T(8,128)(2,1)S(1)}, u32[]{:S(2)}, u32[]{:S(2)}) collective-permute-start(f16[56,432]{1,0:T(8,128)(2,1)S(1)} %slice.254), channel_id=1, source_target_pairs={{0,46},{1,47},{2,32},{3,33},{4,34},{5,35},{6,36},{7,37},{8,38},{9,... | collective-permute-start | bytes 145160 | tf_op jit(solution)/shard_map/ppermute | solution.py:30
  79.7 15.3 %copy-start.1 = (f32[27,6912]{1,0:T(8,128)S(1)}, f32[27,6912]{1,0:T(8,128)}, u32[]{:S(2)}) copy-start(f32[27,6912]{1,0:T(8,128)} %previous.1) | copy-start | bytes 2239492
  80.3 9.2 %collective-permute-start.23 = (f16[56,1296]{1,0:T(8,128)(2,1)S(1)}, f16[56,1296]{1,0:T(8,128)(2,1)S(1)}, u32[]{:S(2)}, u32[]{:S(2)}) collective-permute-start(f16[56,1296]{1,0:T(8,128)(2,1)S(1)} %pad_maximum_fusion.4), channel_id=1, source_target_pairs={{0,14},{1,15},{2,0},{3,1},{4,2},{5,3},{6,4},{7,5},{8,6},{9,7},{10,... | collective-permute-start | bytes 435464 | tf_op jit(solution)/shard_map/ppermute | solution.py:30
  84.1 6.6 %collective-permute-start.14 = (f32[56,432]{1,0:T(8,128)S(1)}, f32[56,432]{1,0:T(8,128)S(1)}, u32[]{:S(2)}, u32[]{:S(2)}) collective-permute-start(f32[56,432]{1,0:T(8,128)S(1)} %get-tuple-element.61), channel_id=1, source_target_pairs={{0,1},{1,0},{2,3},{3,2},{4,5},{5,4},{6,7},{7,6},{8,9},{9,8},{10,11... | collective-permute-start | bytes 290312 | tf_op jit(solution)/shard_map/ppermute | solution.py:30
  91.1 3.9 %collective-permute-start.27 = (f32[27,3456]{1,0:T(8,128)S(1)}, f32[27,3456]{1,0:T(8,128)S(1)}, u32[]{:S(2)}, u32[]{:S(2)}) collective-permute-start(f32[27,3456]{1,0:T(8,128)S(1)} %constant_dynamic-slice_fusion.3), channel_id=1, source_target_pairs={{0,16},{1,17},{2,18},{3,19},{4,20},{5,21},{6,22},{7,23},{8,24},{9,... | collective-permute-start | bytes 1119752 | tf_op jit(solution)/shard_map/ppermute | solution.py:30
